TPU v7x, 32 devices: a whole 2x2x4 slice. The times are simulated.
32 devices in a mesh: dp: 16 (over z, y, core), cout: 2 (over x).
Axes of the slice: x: 2, y: 2, z: 4, core: 2. Of those that a mesh axis runs over, the one named last changes fastest.
Arguments:
- images: bfloat16 [64, 512, 1024], P('dp', 'cout'), may hold values from -6 to 6
- styles: float32 [64, 512], P('dp'), may hold values from -5 to 5
- weight: bfloat16 [9, 512, 512], P(None, 'cout', 'dp'), may hold values from -0.09375 to 0.09375
- cotangent: bfloat16 [64, 512, 1024], P('dp', 'cout'), may hold values from -6 to 6
Outputs:
- output: bfloat16 [64, 512, 1024], P('dp', 'cout')
- input_grad: bfloat16 [64, 512, 1024], P('dp', 'cout')
- style_grad: float32 [64, 512], P('dp', 'cout')
- weight_grad: float32 [9, 512, 512], P(None, 'cout', 'dp')
All inputs are finite; a program needn't handle non-finite values.
Results may differ from a plain program's by a relative error of at most 0.013.
Values may be sent and summed in bfloat16 or wider, within the bound.
A program may use at most 192 MiB of HBM per device.

v0:
```python
import functools
import math

import jax
import jax.numpy as jnp
from jax import lax
from jax.experimental import pallas as pl
from jax.experimental.pallas import tpu as pltpu
from jax.sharding import PartitionSpec as P

epsilon = 1e-08
tap_steps = [(-1, -1), (-1, 0), (-1, 1), (0, -1), (0, 0), (0, 1), (1, -1), (1, 0), (1, 1)]
TAPS = len(tap_steps)
BF16 = jnp.bfloat16
F32 = jnp.float32
HIGHEST = lax.Precision.HIGHEST
LANES = 128
ROWS = 32
VMEM = 56 * 2**20


def shifted(values, row_step, col_step, side, row, column):
    pixels = values.shape[1]
    offset = row_step * side + col_step
    if offset == 0:
        return values
    moved = pltpu.roll(values, (-offset) % pixels, 1)
    inside = None
    for step, place in ((row_step, row), (col_step, column)):
        if step:
            ok = place >= 1 if step < 0 else place < side - 1
            inside = ok if inside is None else inside & ok
    return jnp.where(inside, moved, jnp.zeros_like(moved))


def places(rows, pixels, side):
    pixel = lax.broadcasted_iota(jnp.int32, (rows, pixels), 1)
    return pixel // side, pixel % side


def back_kernel(side, n, me_ref, upstream_ref, factor_ref, weight_ref, *rest):
    out_refs, columns = rest[:n], rest[n]
    outputs, pixels = upstream_ref.shape[1:]
    block = weight_ref.shape[0] // n
    row, column = places(ROWS, pixels, side)

    @pl.loop(0, outputs // ROWS)
    def _(chunk):
        rows = pl.ds(pl.multiple_of(chunk * ROWS, ROWS), ROWS)
        scaled = (upstream_ref[0, rows, :].astype(F32) * factor_ref[0, rows, :]).astype(BF16).astype(F32)
        for tap, (row_step, col_step) in enumerate(tap_steps):
            place = pl.ds(pl.multiple_of(tap * outputs + chunk * ROWS, ROWS), ROWS)
            columns[place, :] = shifted(scaled, -row_step, -col_step, side, row, column).astype(BF16)

    for step in range(n):
        owner = lax.rem(me_ref[0] + step, n)
        rows = pl.ds(pl.multiple_of(owner * block, block), block)
        out_refs[step][0] = jnp.dot(
            weight_ref[rows, :], columns[...], preferred_element_type=F32
        ).astype(BF16)


def forward_kernel(side, n, me_ref, upstream_ref, factor_ref, squares_ref, forward_ref, weight_ref, *rest):
    maps = rest[:n]
    output_ref, energy_ref, gradient_ref, columns, scaled_ref, total = rest[n:]
    outputs, pixels = upstream_ref.shape[1:]
    block = maps[0].shape[1]
    inputs = n * block
    image = pl.program_id(0)
    row, column = places(ROWS, pixels, side)

    @pl.when(image == 0)
    def _():
        total[...] = jnp.zeros_like(total)
        energy_ref[...] = jnp.zeros_like(energy_ref)

    for step in range(n):
        owner = lax.rem(me_ref[0] + n - step, n)

        @pl.loop(0, block // ROWS)
        def _(chunk):
            rows = pl.ds(pl.multiple_of(chunk * ROWS, ROWS), ROWS)
            values = maps[step][0, rows, :].astype(F32)
            for tap, (row_step, col_step) in enumerate(tap_steps):
                place = pl.ds(pl.multiple_of(tap * inputs + owner * block + chunk * ROWS, ROWS), ROWS)
                columns[place, :] = shifted(values, row_step, col_step, side, row, column).astype(BF16)

    factor = factor_ref[0]
    upstream = upstream_ref[0].astype(F32)
    scaled_ref[...] = (upstream * factor).astype(BF16)
    convolved = jnp.dot(forward_ref[...], columns[...], preferred_element_type=F32)
    output_ref[0] = (factor * convolved).astype(BF16)
    norm_grad = jnp.sum(upstream_ref[0].astype(F32) * convolved, axis=1, keepdims=True)
    energy_grad = -0.5 * norm_grad * (factor * factor * factor)
    lane = lax.broadcasted_iota(jnp.int32, energy_ref.shape, 1)
    energy_ref[...] += jnp.where(lane == image, energy_grad, 0.0)

    for tap in range(TAPS):
        total[:, tap * outputs : (tap + 1) * outputs] += lax.dot_general(
            columns[tap * inputs : (tap + 1) * inputs, :],
            scaled_ref[...],
            (((1,), (1,)), ((), ())),
            preferred_element_type=F32,
        )

    @pl.when(image == pl.num_programs(0) - 1)
    def _():
        radial = 2.0 * lax.dot_general(
            squares_ref[...],
            energy_ref[...],
            (((1,), (1,)), ((), ())),
            precision=HIGHEST,
            preferred_element_type=F32,
        )
        for tap in range(TAPS):
            part = slice(tap * outputs, (tap + 1) * outputs)
            gradient_ref[:, part] = (
                total[:, part] + weight_ref[:, part].astype(F32) * radial
            ).astype(BF16)


def on_device(n, images, styles, weight, cotangent):
    batch, block, pixels = images.shape
    outputs = weight.shape[1]
    inputs = styles.shape[1]
    side = math.isqrt(pixels)
    me = lax.axis_index("cout")
    position = me.reshape(1).astype(jnp.int32)

    def send(values, step):
        return lax.ppermute(values, "cout", [(j, (j + step) % n) for j in range(n)])

    local_styles = lax.dynamic_slice_in_dim(styles, me * block, block, 1)
    modulated = (images.astype(F32) * local_styles[:, :, None]).astype(BF16)
    maps = [modulated] + [send(modulated, step) for step in range(1, n)]

    mine = weight.transpose(2, 0, 1).reshape(weight.shape[2], TAPS * outputs)
    by_input = lax.all_gather(mine, "dp", axis=0, tiled=True)
    cube = by_input.reshape(inputs, TAPS, outputs)
    kernel_energy = jnp.sum(jnp.square(cube.astype(F32)), axis=1)
    style_square = styles * styles
    energy = jnp.dot(style_square, kernel_energy, precision=HIGHEST)
    demodulation = lax.rsqrt(energy + epsilon)
    factor = demodulation[:, :, None]
    by_output = cube.transpose(2, 1, 0).reshape(outputs, TAPS * inputs)

    smem = pl.BlockSpec(memory_space=pltpu.SMEM)
    work = 2 * TAPS * inputs * outputs * pixels
    backs = []
    for image in range(batch):
        at = functools.partial(lambda image, i: (image, 0, 0), image)
        parts = pl.pallas_call(
            functools.partial(back_kernel, side, n),
            grid=(1,),
            out_shape=[jax.ShapeDtypeStruct((1, block, pixels), BF16)] * n,
            in_specs=[
                smem,
                pl.BlockSpec((1, outputs, pixels), at),
                pl.BlockSpec((1, outputs, 1), at),
                pl.BlockSpec(by_input.shape, lambda i: (0, 0)),
            ],
            out_specs=[pl.BlockSpec((1, block, pixels), lambda i: (0, 0, 0))] * n,
            scratch_shapes=[pltpu.VMEM((TAPS * outputs, pixels), BF16)],
            compiler_params=pltpu.CompilerParams(vmem_limit_bytes=VMEM),
            cost_estimate=pl.CostEstimate(
                flops=2 * work, bytes_accessed=8 * outputs * pixels, transcendentals=0
            ),
            name="back",
        )(position, cotangent, factor, by_input)
        backs.append([parts[0]] + [send(parts[step], step) for step in range(1, n)])

    lanes = -(-batch // LANES) * LANES
    squares = jnp.pad(style_square.T, ((0, 0), (0, lanes - batch)))
    one = lambda i: (i, 0, 0)
    whole = lambda i: (0, 0)
    output, energy_columns, gradient = pl.pallas_call(
        functools.partial(forward_kernel, side, n),
        grid=(batch,),
        out_shape=[
            jax.ShapeDtypeStruct((batch, outputs, pixels), BF16),
            jax.ShapeDtypeStruct((outputs, lanes), F32),
            jax.ShapeDtypeStruct((inputs, TAPS * outputs), BF16),
        ],
        in_specs=[
            smem,
            pl.BlockSpec((1, outputs, pixels), one),
            pl.BlockSpec((1, outputs, 1), one),
            pl.BlockSpec(squares.shape, whole),
            pl.BlockSpec(by_output.shape, whole),
            pl.BlockSpec(by_input.shape, whole),
        ]
        + [pl.BlockSpec((1, block, pixels), one)] * n,
        out_specs=[
            pl.BlockSpec((1, outputs, pixels), one),
            pl.BlockSpec((outputs, lanes), whole),
            pl.BlockSpec((inputs, TAPS * outputs), whole),
        ],
        scratch_shapes=[
            pltpu.VMEM((TAPS * inputs, pixels), BF16),
            pltpu.VMEM((outputs, pixels), BF16),
            pltpu.VMEM((inputs, TAPS * outputs), F32),
        ],
        compiler_params=pltpu.CompilerParams(vmem_limit_bytes=VMEM),
        cost_estimate=pl.CostEstimate(
            flops=3 * batch * work, bytes_accessed=16 * batch * outputs * pixels, transcendentals=0
        ),
        name="forward",
    )(position, cotangent, factor, squares, by_output, by_input, *maps)

    gradient = lax.psum_scatter(gradient, "dp", scatter_dimension=0, tiled=True)
    image_count = batch * lax.axis_size("dp")
    weight_grad = gradient.astype(F32).reshape(-1, TAPS, outputs).transpose(1, 2, 0) * (1.0 / image_count)

    energy_grad = energy_columns[:, :batch].T
    style_terms = 2.0 * styles * jnp.dot(energy_grad, kernel_energy.T, precision=HIGHEST)
    style_terms = style_terms.astype(BF16)
    style_sum = 0.0
    for step in range(n):
        part = lax.dynamic_slice_in_dim(style_terms, lax.rem(me + step, n) * block, block, 1)
        style_sum = style_sum + (send(part, step) if step else part).astype(F32)

    back_sum = 0.0
    for step in range(n):
        back_sum = back_sum + jnp.concatenate([parts[step] for parts in backs], 0).astype(F32)
    input_grad = (back_sum * local_styles[:, :, None]).astype(BF16)
    style_grad = jnp.sum(back_sum * images.astype(F32), axis=2) + style_sum
    return (output, input_grad, style_grad, weight_grad)


def solution(mesh):
    return jax.shard_map(
        functools.partial(on_device, mesh.shape["cout"]),
        mesh=mesh,
        in_specs=(
            P("dp", "cout", None),
            P("dp", None),
            P(None, "cout", "dp"),
            P("dp", "cout", None),
        ),
        out_specs=(
            P("dp", "cout", None),
            P("dp", "cout", None),
            P("dp", "cout"),
            P(None, "cout", "dp"),
        ),
        check_vma=False,
    )
```

profile of v0, /device:TPU:0, one launch (start us, length us, event | category | flops | bytes accessed | tf_op | source)
XLA Modules:
  0.0 280.9 jit_solution(17555676980093975476)
XLA Ops:
  7.2 1.6 copy.37
  9.7 46.1 %all-gather.2.cloned.1.call-done.weight_ref = bf16[512,2304]{1,0:T(8,128)(2,1)} async-done(((bf16[32,2304]{1,0:T(8,128)(2,1)}), bf16[512,2304]{1,0:T(8,128)(2,1)}) %all-gather.2.cloned.1.call-update) | async-done | bytes 2359312 | tf_op jit(solution)/shard_map/all_gather | solution.py:138
  55.8 2.8 %copy.28 = bf16[512,2304]{0,1:T(8,128)(2,1)S(1)} copy(bf16[512,2304]{1,0:T(8,128)(2,1)} %all-gather.2.cloned.1.call-done.weight_ref) | data formatting | bytes 4718592 | tf_op jit(solution)/shard_map/all_gather | solution.py:138
  59.7 1.1 copy.30.factor_ref
  60.7 7.5 %back.4 = (bf16[1,256,1024]{2,1,0:T(8,128)(2,1)}, bf16[1,256,1024]{2,1,0:T(8,128)(2,1)}) custom-call(s32[1]{0:T(128)} %bitcast.me_ref, bf16[4,256,1024]{2,1,0:T(8,128)(2,1)} %upstream_ref.9, f32[4,256,1]{2,1,0:T(8,128)} %copy.30.factor_ref, bf16[512,2304]{1,0:T(8,128)(2,1)} %all-gather.2.cloned.1.call-done.weight_ref), custom_call_target="tpu_custom_call" | custom-call | flops 4831838208 | bytes 2097152 | tf_op jit(solution)/shard_map/back/pallas_call | solution.py:152
  68.3 1.5 collective-permute-start.1
  69.7 7.6 %back.5 = (bf16[1,256,1024]{2,1,0:T(8,128)(2,1)}, bf16[1,256,1024]{2,1,0:T(8,128)(2,1)}) custom-call(s32[1]{0:T(128)} %bitcast.me_ref, bf16[4,256,1024]{2,1,0:T(8,128)(2,1)} %upstream_ref.9, f32[4,256,1]{2,1,0:T(8,128)} %copy.30.factor_ref, bf16[512,2304]{1,0:T(8,128)(2,1)} %all-gather.2.cloned.1.call-done.weight_ref), custom_call_target="tpu_custom_call" | custom-call | flops 4831838208 | bytes 2097152 | tf_op jit(solution)/shard_map/back/pallas_call | solution.py:152
  77.9 7.6 %back.6 = (bf16[1,256,1024]{2,1,0:T(8,128)(2,1)}, bf16[1,256,1024]{2,1,0:T(8,128)(2,1)}) custom-call(s32[1]{0:T(128)} %bitcast.me_ref, bf16[4,256,1024]{2,1,0:T(8,128)(2,1)} %upstream_ref.9, f32[4,256,1]{2,1,0:T(8,128)} %copy.30.factor_ref, bf16[512,2304]{1,0:T(8,128)(2,1)} %all-gather.2.cloned.1.call-done.weight_ref), custom_call_target="tpu_custom_call" | custom-call | flops 4831838208 | bytes 2097152 | tf_op jit(solution)/shard_map/back/pallas_call | solution.py:152
  85.4 1.5 collective-permute-start.3
  86.9 7.6 %back.7 = (bf16[1,256,1024]{2,1,0:T(8,128)(2,1)}, bf16[1,256,1024]{2,1,0:T(8,128)(2,1)}) custom-call(s32[1]{0:T(128)} %bitcast.me_ref, bf16[4,256,1024]{2,1,0:T(8,128)(2,1)} %upstream_ref.9, f32[4,256,1]{2,1,0:T(8,128)} %copy.30.factor_ref, bf16[512,2304]{1,0:T(8,128)(2,1)} %all-gather.2.cloned.1.call-done.weight_ref), custom_call_target="tpu_custom_call" | custom-call | flops 4831838208 | bytes 2097152 | tf_op jit(solution)/shard_map/back/pallas_call | solution.py:152
  95.0 10.8 %collective-permute-done.3 = bf16[1,256,1024]{2,1,0:T(8,128)(2,1)} collective-permute-done((bf16[1,256,1024]{2,1,0:T(8,128)(2,1)}, bf16[1,256,1024]{2,1,0:T(8,128)(2,1)}, u32[]{:S(2)}, u32[]{:S(2)}) %collective-permute-start.3) | collective-permute-done | bytes 524320 | tf_op jit(solution)/shard_map/ppermute | solution.py:131
  105.8 10.6 %collective-permute-done.4 = bf16[1,256,1024]{2,1,0:T(8,128)(2,1)} collective-permute-done((bf16[1,256,1024]{2,1,0:T(8,128)(2,1)}, bf16[1,256,1024]{2,1,0:T(8,128)(2,1)}, u32[]{:S(2)}, u32[]{:S(2)}) %collective-permute-start.4) | collective-permute-done | bytes 524320 | tf_op jit(solution)/shard_map/ppermute | solution.py:131
  116.4 4.8 %fusion.1 = (f32[4,256]{1,0:T(4,128)S(1)}, bf16[4,256,1024]{2,1,0:T(8,128)(2,1)}, bf16[4,256,1024]{2,1,0:T(8,128)(2,1)}) fusion(bf16[4,256,1024]{2,1,0:T(8,128)(2,1)} %param.4, bf16[1,256,1024]{2,1,0:T(8,128)(2,1)} %collective-permute-done.4, bf16[1,256,1024]{2,1,0:T(8,128)(2,1)} %collective-permute-done.3, bf16[1,256,1024]{2,1,0:T(8,128)(2,1)} %collective-permute-done.2, ...), kind=kLoop, calls=%fused_computation.4 | loop fusion | flops 16776192 | bytes 10493952 | tf_op jit(solution)/shard_map/reduce_sum | solution.py:226
  121.2 1.5 collective-permute-start
  123.4 2.5 copy.29
  125.9 4.3 %copy.31.forward_ref = bf16[256,4608]{1,0:T(8,128)(2,1)} copy(bf16[256,4608]{0,1:T(8,128)(2,1)} %bitcast.17) | data formatting | bytes 4718592 | tf_op jit(solution)/shard_map/reshape | solution.py:145
  130.2 38.3 %collective-permute-done.rest_1_ = bf16[4,256,1024]{2,1,0:T(8,128)(2,1)} collective-permute-done((bf16[4,256,1024]{2,1,0:T(8,128)(2,1)}, bf16[4,256,1024]{2,1,0:T(8,128)(2,1)}, u32[]{:S(2)}, u32[]{:S(2)}) %collective-permute-start) | collective-permute-done | bytes 2097184 | tf_op jit(solution)/shard_map/ppermute | solution.py:131
  168.5 41.7 %forward.1 = (bf16[4,256,1024]{2,1,0:T(8,128)(2,1)}, f32[256,128]{1,0:T(8,128)}, bf16[512,2304]{1,0:T(8,128)(2,1)}) custom-call(s32[1]{0:T(128)} %bitcast.me_ref, bf16[4,256,1024]{2,1,0:T(8,128)(2,1)} %upstream_ref.9, f32[4,256,1]{2,1,0:T(8,128)} %copy.30.factor_ref, f32[512,128]{1,0:T(8,128)} %pad.4.squares_ref, bf16[256,4608]{1,0:T(8,128)(2,1)} %copy.31.forward_ref, ...), custom_call_target="tpu_custom_call" | custom-call | flops 28991029248 | bytes 16777216 | tf_op jit(solution)/shard_map/forward/pallas_call | solution.py:176
  210.3 0.9 copy-done
  211.5 1.5 collective-permute-start.5
  213.0 2.1 collective-permute-done.5
  215.8 56.4 %reduce-scatter.2.cloned.1.call-done = bf16[32,2304]{1,0:T(8,128)(2,1)} async-done(((bf16[512,2304]{1,0:T(8,128)(2,1)}), bf16[32,2304]{1,0:T(8,128)(2,1)}) %reduce-scatter.2.cloned.1.call-update) | async-done | bytes 147472 | tf_op jit(solution)/shard_map/reduce_scatter | solution.py:210
  272.2 0.9 convert_multiply_fusion.2
  273.2 0.9 copy.36
  (21 shorter events, 4.9 us)
Async XLA Ops:
  7.2 48.6 %all-gather.2.cloned.1.call-start = ((), (), s32[]{:S(2)}) async-start(), calls=%async_computation.1 | async-start | bytes 2506752 | tf_op jit(solution)/shard_map/all_gather | solution.py:138
  8.8 263.3 %reduce-scatter.2.cloned.1.call-start = ((), (), s32[]{:S(2)}) async-start(), calls=%async_computation.2 | async-start | bytes 2506752 | tf_op jit(solution)/shard_map/reduce_scatter | solution.py:210
  68.3 26.7 %collective-permute-start.1 = (bf16[1,256,1024]{2,1,0:T(8,128)(2,1)}, bf16[1,256,1024]{2,1,0:T(8,128)(2,1)}, u32[]{:S(2)}, u32[]{:S(2)}) collective-permute-start(bf16[1,256,1024]{2,1,0:T(8,128)(2,1)} %get-tuple-element.20), channel_id=1, source_target_pairs={{0,1},{1,0},{2,3},{3,2},{4,5},{5,4},{6,7},{7,6},{8,9},{9,8},{10,11... | collective-permute-start | bytes 1572872 | tf_op jit(solution)/shard_map/ppermute | solution.py:131
  77.3 17.7 %collective-permute-start.2 = (bf16[1,256,1024]{2,1,0:T(8,128)(2,1)}, bf16[1,256,1024]{2,1,0:T(8,128)(2,1)}, u32[]{:S(2)}, u32[]{:S(2)}) collective-permute-start(bf16[1,256,1024]{2,1,0:T(8,128)(2,1)} %get-tuple-element.21), channel_id=1, source_target_pairs={{0,1},{1,0},{2,3},{3,2},{4,5},{5,4},{6,7},{7,6},{8,9},{9,8},{10,11... | collective-permute-start | bytes 1572872 | tf_op jit(solution)/shard_map/ppermute | solution.py:131
  85.4 9.6 %copy-start.1 = (f32[4,512]{1,0:T(4,128)S(1)}, f32[4,512]{1,0:T(4,128)}, u32[]{:S(2)}) copy-start(f32[4,512]{1,0:T(4,128)} %param.5) | copy-start | bytes 24580
  85.4 20.4 %collective-permute-start.3 = (bf16[1,256,1024]{2,1,0:T(8,128)(2,1)}, bf16[1,256,1024]{2,1,0:T(8,128)(2,1)}, u32[]{:S(2)}, u32[]{:S(2)}) collective-permute-start(bf16[1,256,1024]{2,1,0:T(8,128)(2,1)} %get-tuple-element.22), channel_id=1, source_target_pairs={{0,1},{1,0},{2,3},{3,2},{4,5},{5,4},{6,7},{7,6},{8,9},{9,8},{10,11... | collective-permute-start | bytes 1572872 | tf_op jit(solution)/shard_map/ppermute | solution.py:131
  94.4 21.9 %collective-permute-start.4 = (bf16[1,256,1024]{2,1,0:T(8,128)(2,1)}, bf16[1,256,1024]{2,1,0:T(8,128)(2,1)}, u32[]{:S(2)}, u32[]{:S(2)}) collective-permute-start(bf16[1,256,1024]{2,1,0:T(8,128)(2,1)} %get-tuple-element.23), channel_id=1, source_target_pairs={{0,1},{1,0},{2,3},{3,2},{4,5},{5,4},{6,7},{7,6},{8,9},{9,8},{10,11... | collective-permute-start | bytes 1572872 | tf_op jit(solution)/shard_map/ppermute | solution.py:131
  121.2 47.3 %collective-permute-start = (bf16[4,256,1024]{2,1,0:T(8,128)(2,1)}, bf16[4,256,1024]{2,1,0:T(8,128)(2,1)}, u32[]{:S(2)}, u32[]{:S(2)}) collective-permute-start(bf16[4,256,1024]{2,1,0:T(8,128)(2,1)} %get-tuple-element.36.rest_0_), channel_id=1, source_target_pairs={{0,1},{1,0},{2,3},{3,2},{4,5},{5,4},{6,7},{7,6},{8,9},{9,8},{10,11... | collective-permute-start | bytes 6291464 | tf_op jit(solution)/shard_map/ppermute | solution.py:131
  210.2 0.9 copy-start
  211.5 3.6 %collective-permute-start.5 = (bf16[4,256]{1,0:T(4,128)(2,1)S(1)}, bf16[4,256]{1,0:T(4,128)(2,1)S(1)}, u32[]{:S(2)}, u32[]{:S(2)}) collective-permute-start(bf16[4,256]{1,0:T(4,128)(2,1)S(1)} %constant_dynamic-slice_fusion), channel_id=1, source_target_pairs={{0,1},{1,0},{2,3},{3,2},{4,5},{5,4},{6,7},{7,6},{8,9},{9,8},{10,11... | collective-permute-start | bytes 6152 | tf_op jit(solution)/shard_map/ppermute | solution.py:131
Sparse Core Ops, SparseCore 0:
  10.9 44.9 all-gather.1
  210.4 61.7 reduce-scatter.1
where the time goes:
time: 281 us
  waiting for transfers between devices  164 us (58%)
  Pallas kernels  72 us (26%)
  local copies, waits for them, and re-layouts  15.6 us (6%)
  between operations  14.1 us (5%)
  starting transfers between devices  7.13 us (3%)
  other arithmetic  6.85 us (2%)
    ppermute x6, waiting for transfers between devices, send(): return lax.ppermute(values, 'cout', [(j, (j + step) % n) for j in range(n)])  61.8 us
    reduce_scatter x1, waiting for transfers between devices, on_device(): gradient = lax.psum_scatter(gradient, 'dp', scatter_dimension=0, tiled=True)  56.4 us
    all_gather x1, waiting for transfers between devices, on_device(): by_input = lax.all_gather(mine, 'dp', axis=0, tiled=True)  46.1 us
    pallas_call x1, Pallas kernels, on_device(): pl.pallas_call(functools.partial(forward_kernel, side, n), grid=(batch,),...  41.7 us
    pallas_call x4, Pallas kernels, on_device(): pl.pallas_call(functools.partial(back_kernel, side, n), grid=(1,), out_sh...  30.2 us
    ppermute x6, starting transfers between devices, send(): return lax.ppermute(values, 'cout', [(j, (j + step) % n) for j in range(n)])  7.04 us
  transfers between devices with their start and end apart: 8, of which 6 were waited for; matrix products, arithmetic and copies ran while one was open for 3% of the time, Pallas kernels for 8%

commit v1 on v0

--- a/solution.py
+++ b/solution.py
@@ -17,6 +17,7 @@
 LANES = 128
 ROWS = 32
 VMEM = 56 * 2**20
+MESH = pl.DeviceIdType.MESH
 
 
 def shifted(values, row_step, col_step, side, row, column):
@@ -39,7 +40,7 @@
 
 
 def back_kernel(side, n, me_ref, upstream_ref, factor_ref, weight_ref, *rest):
-    out_refs, columns = rest[:n], rest[n]
+    out_refs, columns, terms = rest[:n], rest[n], rest[n + 1]
     outputs, pixels = upstream_ref.shape[1:]
     block = weight_ref.shape[0] // n
     row, column = places(ROWS, pixels, side)
@@ -47,22 +48,20 @@
     @pl.loop(0, outputs // ROWS)
     def _(chunk):
         rows = pl.ds(pl.multiple_of(chunk * ROWS, ROWS), ROWS)
-        scaled = (upstream_ref[0, rows, :].astype(F32) * factor_ref[0, rows, :]).astype(BF16).astype(F32)
+        scaled = (upstream_ref[0, rows, :].astype(F32) * factor_ref[0, rows, :]).astype(BF16)
         for tap, (row_step, col_step) in enumerate(tap_steps):
             place = pl.ds(pl.multiple_of(tap * outputs + chunk * ROWS, ROWS), ROWS)
             columns[place, :] = shifted(scaled, -row_step, -col_step, side, row, column).astype(BF16)
 
+    terms[...] = jnp.dot(weight_ref[...], columns[...], preferred_element_type=F32).astype(BF16)
     for step in range(n):
         owner = lax.rem(me_ref[0] + step, n)
-        rows = pl.ds(pl.multiple_of(owner * block, block), block)
-        out_refs[step][0] = jnp.dot(
-            weight_ref[rows, :], columns[...], preferred_element_type=F32
-        ).astype(BF16)
-
-
-def forward_kernel(side, n, me_ref, upstream_ref, factor_ref, squares_ref, forward_ref, weight_ref, *rest):
+        out_refs[step][0] = terms[pl.ds(pl.multiple_of(owner * block, block), block), :]
+
+
+def forward_kernel(side, n, me_ref, upstream_ref, factor_ref, squares_ref, weight_ref, *rest):
     maps = rest[:n]
-    output_ref, energy_ref, gradient_ref, columns, scaled_ref, total = rest[n:]
+    output_ref, energy_ref, gradient_ref, columns, scaled_ref, forward_ref, total = rest[n:]
     outputs, pixels = upstream_ref.shape[1:]
     block = maps[0].shape[1]
     inputs = n * block
@@ -71,6 +70,8 @@
 
     @pl.when(image == 0)
     def _():
+        for tap in range(TAPS):
+            forward_ref[:, tap * inputs : (tap + 1) * inputs] = weight_ref[:, tap * outputs : (tap + 1) * outputs].T
         total[...] = jnp.zeros_like(total)
         energy_ref[...] = jnp.zeros_like(energy_ref)
 
@@ -80,7 +81,7 @@
         @pl.loop(0, block // ROWS)
         def _(chunk):
             rows = pl.ds(pl.multiple_of(chunk * ROWS, ROWS), ROWS)
-            values = maps[step][0, rows, :].astype(F32)
+            values = maps[step][0, rows, :]
             for tap, (row_step, col_step) in enumerate(tap_steps):
                 place = pl.ds(pl.multiple_of(tap * inputs + owner * block + chunk * ROWS, ROWS), ROWS)
                 columns[place, :] = shifted(values, row_step, col_step, side, row, column).astype(BF16)
@@ -95,9 +96,10 @@
     lane = lax.broadcasted_iota(jnp.int32, energy_ref.shape, 1)
     energy_ref[...] += jnp.where(lane == image, energy_grad, 0.0)
 
-    for tap in range(TAPS):
-        total[:, tap * outputs : (tap + 1) * outputs] += lax.dot_general(
-            columns[tap * inputs : (tap + 1) * inputs, :],
+    group = 3 * inputs
+    for at in range(0, TAPS * inputs, group):
+        total[at : at + group, :] += lax.dot_general(
+            columns[at : at + group, :],
             scaled_ref[...],
             (((1,), (1,)), ((), ())),
             preferred_element_type=F32,
@@ -115,8 +117,160 @@
         for tap in range(TAPS):
             part = slice(tap * outputs, (tap + 1) * outputs)
             gradient_ref[:, part] = (
-                total[:, part] + weight_ref[:, part].astype(F32) * radial
+                total[tap * inputs : (tap + 1) * inputs, :] + weight_ref[:, part].astype(F32) * radial
             ).astype(BF16)
+
+
+def flipped(me, distances):
+    place = me
+    for distance in distances:
+        place = place + distance * (1 - 2 * lax.rem(lax.div(me, distance), 2))
+    return place
+
+
+def orders(size, columns):
+    distances = [1 << bit for bit in range(size.bit_length() - 1)][::-1]
+    if columns % (2 * LANES) or size < 8:
+        return [(slice(0, columns), distances)]
+    half = columns // 2
+    turned = distances[-2:-1] + distances[:-2] + distances[-1:]
+    return [(slice(0, half), distances), (slice(half, columns), turned)]
+
+
+def distances_of(order, slot):
+    return [distance for bit, distance in enumerate(order) if (slot >> bit) & 1]
+
+
+def greet(me, order):
+    barrier = pltpu.get_barrier_semaphore()
+    for distance in order:
+        pl.semaphore_signal(barrier, inc=1, device_id={"dp": flipped(me, [distance])}, device_id_type=MESH)
+    pl.semaphore_wait(barrier, len(order))
+
+
+def gather_kernel(size, parts, taps, mine_ref, after_ref, whole_ref, energy_ref, send_sem, recv_sem, *held):
+    me = lax.axis_index("dp")
+    del after_ref
+    steps = len(parts[0][1])
+    for part, (columns, _) in enumerate(parts):
+        held[part][0] = mine_ref[:, columns]
+    greet(me, parts[0][1])
+    copies = [None] * len(parts)
+    for step in range(steps):
+        for part, (_, order) in enumerate(parts):
+            if step:
+                copies[part].wait()
+            count = 1 << step
+            copies[part] = pltpu.make_async_remote_copy(
+                src_ref=held[part].at[0:count],
+                dst_ref=held[part].at[count : 2 * count],
+                send_sem=send_sem.at[part, step],
+                recv_sem=recv_sem.at[part, step],
+                device_id={"dp": flipped(me, [order[step]])},
+                device_id_type=MESH,
+            )
+            copies[part].start()
+    for copy in copies:
+        copy.wait()
+    outputs = energy_ref.shape[2]
+    for part, (columns, order) in enumerate(parts):
+        for slot in range(size):
+            owner = flipped(me, distances_of(order, slot))
+            whole_ref[owner, :, columns] = held[part][slot]
+    for slot in range(size):
+        energy = None
+        for tap in range(taps):
+            value = whole_ref[slot, :, tap * outputs : (tap + 1) * outputs].astype(F32)
+            energy = value * value if energy is None else energy + value * value
+        energy_ref[slot] = energy
+
+
+def reduce_kernel(size, parts, terms_ref, total_ref, send_sem, recv_sem, *scratch):
+    me = lax.axis_index("dp")
+    steps = len(parts[0][1])
+    work, came = scratch[: len(parts)], scratch[len(parts) :]
+    greet(me, parts[0][1])
+    copies = [None] * len(parts)
+    for step in range(steps - 1, -1, -1):
+        count = 1 << step
+        for part, (columns, order) in enumerate(parts):
+            if step == steps - 1:
+                for slot in range(size):
+                    owner = flipped(me, distances_of(order, slot))
+                    work[part][slot] = terms_ref[owner, :, columns]
+            else:
+                copies[part].wait()
+                for slot in range(2 * count):
+                    work[part][slot] = (
+                        work[part][slot].astype(F32) + came[part][2 * count + slot].astype(F32)
+                    ).astype(BF16)
+            copies[part] = pltpu.make_async_remote_copy(
+                src_ref=work[part].at[count : 2 * count],
+                dst_ref=came[part].at[count : 2 * count],
+                send_sem=send_sem.at[part, step],
+                recv_sem=recv_sem.at[part, step],
+                device_id={"dp": flipped(me, [order[step]])},
+                device_id_type=MESH,
+            )
+            copies[part].start()
+    for part, (columns, _) in enumerate(parts):
+        copies[part].wait()
+        total_ref[:, columns] = work[part][0].astype(F32) + came[part][1].astype(F32)
+
+
+def modulate_kernel(images_ref, styles_ref, modulated_ref):
+    modulated_ref[...] = (images_ref[...].astype(F32) * styles_ref[...]).astype(BF16)
+
+
+def finish_kernel(n, after_ref, images_ref, styles_ref, *rest):
+    del after_ref
+    parts, (input_ref, style_ref) = rest[:-2], rest[-2:]
+    for image in range(images_ref.shape[0]):
+        total = 0.0
+        for part in parts[image * n : (image + 1) * n]:
+            total = total + part[0].astype(F32)
+        input_ref[image] = (total * styles_ref[image]).astype(BF16)
+        style_ref[image] = jnp.sum(total * images_ref[image].astype(F32), axis=1, keepdims=True)
+
+
+def exchange_scratch(size, parts, rows, buffers):
+    steps = len(parts[0][1])
+    return [pltpu.SemaphoreType.DMA((len(parts), steps))] * 2 + [
+        pltpu.VMEM((size, rows, columns.stop - columns.start), BF16) for columns, _ in parts
+    ] * buffers
+
+
+def gather_rows(mine, after, size):
+    rows, columns = mine.shape
+    parts = orders(size, columns)
+    vmem = pl.BlockSpec(memory_space=pltpu.VMEM)
+    return pl.pallas_call(
+        functools.partial(gather_kernel, size, parts, TAPS),
+        out_shape=[
+            jax.ShapeDtypeStruct((size, rows, columns), BF16),
+            jax.ShapeDtypeStruct((size, rows, columns // TAPS), F32),
+        ],
+        in_specs=[vmem, pl.BlockSpec(memory_space=pl.ANY)],
+        out_specs=[vmem, vmem],
+        scratch_shapes=exchange_scratch(size, parts, rows, 1),
+        compiler_params=pltpu.CompilerParams(collective_id=0, has_side_effects=True, vmem_limit_bytes=VMEM),
+        name="gather",
+    )(mine, after)
+
+
+def reduce_rows(terms, size):
+    _, rows, columns = terms.shape
+    parts = orders(size, columns)
+    vmem = pl.BlockSpec(memory_space=pltpu.VMEM)
+    return pl.pallas_call(
+        functools.partial(reduce_kernel, size, parts),
+        out_shape=jax.ShapeDtypeStruct((rows, columns), F32),
+        in_specs=[vmem],
+        out_specs=vmem,
+        scratch_shapes=exchange_scratch(size, parts, rows, 2),
+        compiler_params=pltpu.CompilerParams(collective_id=1, has_side_effects=True, vmem_limit_bytes=VMEM),
+        name="reduce",
+    )(terms)
 
 
 def on_device(n, images, styles, weight, cotangent):
@@ -131,18 +285,29 @@
         return lax.ppermute(values, "cout", [(j, (j + step) % n) for j in range(n)])
 
     local_styles = lax.dynamic_slice_in_dim(styles, me * block, block, 1)
-    modulated = (images.astype(F32) * local_styles[:, :, None]).astype(BF16)
+    vmem = pl.BlockSpec(memory_space=pltpu.VMEM)
+    plan = pltpu.CompilerParams(vmem_limit_bytes=VMEM)
+    one_image = pl.BlockSpec((1, block, pixels), lambda i: (i, 0, 0))
+    modulated = pl.pallas_call(
+        modulate_kernel,
+        grid=(batch,),
+        out_shape=jax.ShapeDtypeStruct(images.shape, BF16),
+        in_specs=[one_image, pl.BlockSpec((1, block, 1), lambda i: (i, 0, 0))],
+        out_specs=one_image,
+        compiler_params=plan,
+        name="modulate",
+    )(images, local_styles[:, :, None])
     maps = [modulated] + [send(modulated, step) for step in range(1, n)]
 
     mine = weight.transpose(2, 0, 1).reshape(weight.shape[2], TAPS * outputs)
-    by_input = lax.all_gather(mine, "dp", axis=0, tiled=True)
-    cube = by_input.reshape(inputs, TAPS, outputs)
-    kernel_energy = jnp.sum(jnp.square(cube.astype(F32)), axis=1)
+    size = lax.axis_size("dp")
+    by_input, kernel_energy = gather_rows(mine, modulated, size)
+    by_input = by_input.reshape(inputs, TAPS * outputs)
+    kernel_energy = kernel_energy.reshape(inputs, outputs)
     style_square = styles * styles
     energy = jnp.dot(style_square, kernel_energy, precision=HIGHEST)
     demodulation = lax.rsqrt(energy + epsilon)
     factor = demodulation[:, :, None]
-    by_output = cube.transpose(2, 1, 0).reshape(outputs, TAPS * inputs)
 
     smem = pl.BlockSpec(memory_space=pltpu.SMEM)
     work = 2 * TAPS * inputs * outputs * pixels
@@ -160,11 +325,9 @@
                 pl.BlockSpec(by_input.shape, lambda i: (0, 0)),
             ],
             out_specs=[pl.BlockSpec((1, block, pixels), lambda i: (0, 0, 0))] * n,
-            scratch_shapes=[pltpu.VMEM((TAPS * outputs, pixels), BF16)],
+            scratch_shapes=[pltpu.VMEM((TAPS * outputs, pixels), BF16), pltpu.VMEM((inputs, pixels), BF16)],
             compiler_params=pltpu.CompilerParams(vmem_limit_bytes=VMEM),
-            cost_estimate=pl.CostEstimate(
-                flops=2 * work, bytes_accessed=8 * outputs * pixels, transcendentals=0
-            ),
+            cost_estimate=pl.CostEstimate(flops=work, bytes_accessed=8 * outputs * pixels, transcendentals=0),
             name="back",
         )(position, cotangent, factor, by_input)
         backs.append([parts[0]] + [send(parts[step], step) for step in range(1, n)])
@@ -186,7 +349,6 @@
             pl.BlockSpec((1, outputs, pixels), one),
             pl.BlockSpec((1, outputs, 1), one),
             pl.BlockSpec(squares.shape, whole),
-            pl.BlockSpec(by_output.shape, whole),
             pl.BlockSpec(by_input.shape, whole),
         ]
         + [pl.BlockSpec((1, block, pixels), one)] * n,
@@ -198,18 +360,19 @@
         scratch_shapes=[
             pltpu.VMEM((TAPS * inputs, pixels), BF16),
             pltpu.VMEM((outputs, pixels), BF16),
-            pltpu.VMEM((inputs, TAPS * outputs), F32),
+            pltpu.VMEM((outputs, TAPS * inputs), BF16),
+            pltpu.VMEM((TAPS * inputs, outputs), F32),
         ],
         compiler_params=pltpu.CompilerParams(vmem_limit_bytes=VMEM),
         cost_estimate=pl.CostEstimate(
-            flops=3 * batch * work, bytes_accessed=16 * batch * outputs * pixels, transcendentals=0
+            flops=2 * batch * work, bytes_accessed=16 * batch * outputs * pixels, transcendentals=0
         ),
         name="forward",
-    )(position, cotangent, factor, squares, by_output, by_input, *maps)
-
-    gradient = lax.psum_scatter(gradient, "dp", scatter_dimension=0, tiled=True)
+    )(position, cotangent, factor, squares, by_input, *maps)
+
+    gradient = reduce_rows(gradient.reshape(size, inputs // size, TAPS * outputs), size)
     image_count = batch * lax.axis_size("dp")
-    weight_grad = gradient.astype(F32).reshape(-1, TAPS, outputs).transpose(1, 2, 0) * (1.0 / image_count)
+    weight_grad = gradient.reshape(-1, TAPS, outputs).transpose(1, 2, 0) * (1.0 / image_count)
 
     energy_grad = energy_columns[:, :batch].T
     style_terms = 2.0 * styles * jnp.dot(energy_grad, kernel_energy.T, precision=HIGHEST)
@@ -219,11 +382,18 @@
         part = lax.dynamic_slice_in_dim(style_terms, lax.rem(me + step, n) * block, block, 1)
         style_sum = style_sum + (send(part, step) if step else part).astype(F32)
 
-    back_sum = 0.0
-    for step in range(n):
-        back_sum = back_sum + jnp.concatenate([parts[step] for parts in backs], 0).astype(F32)
-    input_grad = (back_sum * local_styles[:, :, None]).astype(BF16)
-    style_grad = jnp.sum(back_sum * images.astype(F32), axis=2) + style_sum
+    input_grad, style_part = pl.pallas_call(
+        functools.partial(finish_kernel, n),
+        out_shape=[
+            jax.ShapeDtypeStruct(images.shape, BF16),
+            jax.ShapeDtypeStruct((batch, block, 1), F32),
+        ],
+        in_specs=[pl.BlockSpec(memory_space=pl.ANY)] + [vmem] * (2 + n * batch),
+        out_specs=[vmem, vmem],
+        compiler_params=plan,
+        name="finish",
+    )(gradient, images, local_styles[:, :, None], *[part for parts in backs for part in parts])
+    style_grad = style_part[:, :, 0] + style_sum
     return (output, input_grad, style_grad, weight_grad)
 
 

time: 281 us -> 158 us (0.56)
  waiting for transfers between devices: 164 us -> 0.02 us
  Pallas kernels: 72 us -> 137 us
  between operations: 14.1 us -> 0.78 us
  local copies, waits for them, and re-layouts: 15.6 us -> 6.55 us
  other arithmetic: 6.85 us -> 2.86 us
    pallas_call x0 -> x4, Pallas kernels: none -> 65.6 us  [the longest x1 28.1 us: reduce_rows(): pl.pallas_call(functools.partial(reduce_kernel, size, parts), out_shape=j...]
    ppermute x6, waiting for transfers between devices: 61.8 us -> 0.02 us  [send(): return lax.ppermute(values, 'cout', [(j, (j + step) % n) for j in range(n)])]
    reduce_scatter x1 -> x0, waiting for transfers between devices: 56.4 us -> none  [on_device(): gradient = lax.psum_scatter(gradient, 'dp', scatter_dimension=0, tiled=True)]
    all_gather x1 -> x0, waiting for transfers between devices: 46.1 us -> none  [on_device(): by_input = lax.all_gather(mine, 'dp', axis=0, tiled=True)]
    reduce_sum x2 -> x0, other arithmetic: 5.3 us -> none  [the longest x1 4.82 us: on_device(): style_grad = jnp.sum(back_sum * images.astype(F32), axis=2) + style_sum]
    reshape x1 -> x0, local copies, waits for them, and re-layouts: 4.3 us -> none  [on_device(): by_output = cube.transpose(2, 1, 0).reshape(outputs, TAPS * inputs)]
    all_gather x1 -> x0, local copies, waits for them, and re-layouts: 2.84 us -> none  [on_device(): by_input = lax.all_gather(mine, 'dp', axis=0, tiled=True)]
  transfers between devices with their start and end apart: 8 -> 6, of which waited for: 6 -> 0; matrix products, arithmetic and copies ran while one was open for 3% -> 5% of each run, Pallas kernels for 8% -> 85%
where the time goes in v1:
time: 158 us; the launch traced here: 157 us
  Pallas kernels  137 us (87%)
  starting transfers between devices  7.61 us (5%)
  local copies, waits for them, and re-layouts  6.55 us (4%)
  other arithmetic  2.86 us (2%)
  matrix products  2.15 us (1%)
    pallas_call x1, Pallas kernels, on_device(): pl.pallas_call(functools.partial(forward_kernel, side, n), grid=(batch,),...  40.1 us
    pallas_call x4, Pallas kernels, on_device(): pl.pallas_call(functools.partial(back_kernel, side, n), grid=(1,), out_sh...  31.5 us
    pallas_call x1, Pallas kernels, reduce_rows(): pl.pallas_call(functools.partial(reduce_kernel, size, parts), out_shape=j...  28.1 us
    pallas_call x1, Pallas kernels, gather_rows(): pl.pallas_call(functools.partial(gather_kernel, size, parts, TAPS), out_s...  27.8 us
    ppermute x6, starting transfers between devices, send(): return lax.ppermute(values, 'cout', [(j, (j + step) % n) for j in range(n)])  7.61 us
    pallas_call x1, Pallas kernels, on_device(): pl.pallas_call(functools.partial(finish_kernel, n), out_shape=[jax.ShapeD...  5.51 us
    pallas_call x1, Pallas kernels, on_device(): pl.pallas_call(modulate_kernel, grid=(batch,), out_shape=jax.ShapeDtypeSt...  4.13 us
  transfers between devices with their start and end apart: 6, of which 0 were waited for; matrix products, arithmetic and copies ran while one was open for 5% of the time, Pallas kernels for 85%

profile of v1, /device:TPU:0, one launch (start us, length us, event | category | flops | bytes accessed | tf_op | source)
XLA Modules:
  0.0 157.2 jit_solution(4297846971245549737)
XLA Ops:
  0.6 0.7 dynamic-slice_bitcast_fusion
  1.3 1.0 copy.15.styles_ref
  2.4 4.1 %modulate.1.after_ref.rest_0_ = bf16[4,256,1024]{2,1,0:T(8,128)(2,1)} custom-call(bf16[4,256,1024]{2,1,0:T(8,128)(2,1)} %images_ref.3, f32[4,256,1]{2,1,0:T(8,128)} %copy.15.styles_ref), custom_call_target="tpu_custom_call" | custom-call | tf_op jit(solution)/shard_map/modulate/pallas_call | solution.py:291
  6.5 2.9 %collective-permute-start = (bf16[4,256,1024]{2,1,0:T(8,128)(2,1)}, bf16[4,256,1024]{2,1,0:T(8,128)(2,1)}, u32[]{:S(2)}, u32[]{:S(2)}) collective-permute-start(bf16[4,256,1024]{2,1,0:T(8,128)(2,1)} %modulate.1.after_ref.rest_0_), channel_id=1, source_target_pairs={{0,1},{1,0},{2,3},{3,2},{4,5},{5,4},{6,7},{7,6},{8,9},{9,8},{10,11... | collective-permute-start | bytes 6291464 | tf_op jit(solution)/shard_map/ppermute | solution.py:285
  9.6 0.7 copy.23
  10.3 27.8 %gather.1 = (bf16[16,32,2304]{2,1,0:T(8,128)(2,1)}, f32[16,32,256]{2,1,0:T(8,128)}) custom-call(bf16[32,2304]{1,0:T(8,128)(2,1)} %bitcast.20, bf16[4,256,1024]{2,1,0:T(8,128)(2,1)} %modulate.1.after_ref.rest_0_), custom_call_target="tpu_custom_call" | custom-call | tf_op jit(solution)/shard_map/gather/pallas_call | solution.py:247
  38.1 1.6 %fusion.2 = f32[4,256,1]{1,0,2:T(4,128)S(1)} fusion(f32[512,256]{1,0:T(8,128)} %bitcast.17, f32[4,512]{0,1:T(8,128)S(1)} %copy.12), kind=kOutput, calls=%fused_computation.4 | convolution fusion | flops 6294528 | bytes 536576 | tf_op jit(solution)/shard_map/dot_general | solution.py:308
  39.7 1.1 copy.16.factor_ref
  40.8 7.9 %back.4 = (bf16[1,256,1024]{2,1,0:T(8,128)(2,1)}, bf16[1,256,1024]{2,1,0:T(8,128)(2,1)}) custom-call(s32[1]{0:T(128)} %bitcast.me_ref, bf16[4,256,1024]{2,1,0:T(8,128)(2,1)} %upstream_ref.9, f32[4,256,1]{2,1,0:T(8,128)} %copy.16.factor_ref, bf16[512,2304]{1,0:T(8,128)(2,1)} %bitcast.22), custom_call_target="tpu_custom_call" | custom-call | flops 2415919104 | bytes 2097152 | tf_op jit(solution)/shard_map/back/pallas_call | solution.py:317
  49.2 7.9 %back.5 = (bf16[1,256,1024]{2,1,0:T(8,128)(2,1)}, bf16[1,256,1024]{2,1,0:T(8,128)(2,1)}) custom-call(s32[1]{0:T(128)} %bitcast.me_ref, bf16[4,256,1024]{2,1,0:T(8,128)(2,1)} %upstream_ref.9, f32[4,256,1]{2,1,0:T(8,128)} %copy.16.factor_ref, bf16[512,2304]{1,0:T(8,128)(2,1)} %bitcast.23), custom_call_target="tpu_custom_call" | custom-call | flops 2415919104 | bytes 2097152 | tf_op jit(solution)/shard_map/back/pallas_call | solution.py:317
  57.1 1.5 collective-permute-start.2
  58.6 7.9 %back.6 = (bf16[1,256,1024]{2,1,0:T(8,128)(2,1)}, bf16[1,256,1024]{2,1,0:T(8,128)(2,1)}) custom-call(s32[1]{0:T(128)} %bitcast.me_ref, bf16[4,256,1024]{2,1,0:T(8,128)(2,1)} %upstream_ref.9, f32[4,256,1]{2,1,0:T(8,128)} %copy.16.factor_ref, bf16[512,2304]{1,0:T(8,128)(2,1)} %bitcast.24), custom_call_target="tpu_custom_call" | custom-call | flops 2415919104 | bytes 2097152 | tf_op jit(solution)/shard_map/back/pallas_call | solution.py:317
  67.0 7.8 %back.7 = (bf16[1,256,1024]{2,1,0:T(8,128)(2,1)}, bf16[1,256,1024]{2,1,0:T(8,128)(2,1)}) custom-call(s32[1]{0:T(128)} %bitcast.me_ref, bf16[4,256,1024]{2,1,0:T(8,128)(2,1)} %upstream_ref.9, f32[4,256,1]{2,1,0:T(8,128)} %copy.16.factor_ref, bf16[512,2304]{1,0:T(8,128)(2,1)} %bitcast.25), custom_call_target="tpu_custom_call" | custom-call | flops 2415919104 | bytes 2097152 | tf_op jit(solution)/shard_map/back/pallas_call | solution.py:317
  74.9 1.5 collective-permute-start.4
  76.4 0.7 pad.4.squares_ref
  77.1 40.1 %forward.1 = (bf16[4,256,1024]{2,1,0:T(8,128)(2,1)}, f32[256,128]{1,0:T(8,128)}, bf16[512,2304]{1,0:T(8,128)(2,1)}) custom-call(s32[1]{0:T(128)} %bitcast.me_ref, bf16[4,256,1024]{2,1,0:T(8,128)(2,1)} %upstream_ref.9, f32[4,256,1]{2,1,0:T(8,128)} %copy.16.factor_ref, f32[512,128]{1,0:T(8,128)} %pad.4.squares_ref, bf16[512,2304]{1,0:T(8,128)(2,1)} %bitcast.26, ...), custom_call_target="tpu_custom_call" | custom-call | flops 19327352832 | bytes 16777216 | tf_op jit(solution)/shard_map/forward/pallas_call | solution.py:339
  117.3 28.1 %reduce.2.after_ref = f32[32,2304]{1,0:T(8,128)} custom-call(bf16[16,32,2304]{2,1,0:T(8,128)(2,1)} %bitcast.16), custom_call_target="tpu_custom_call" | custom-call | tf_op jit(solution)/shard_map/reduce/pallas_call | solution.py:265
  146.0 0.6 collective-permute-start.5
  146.6 1.0 broadcast_multiply_fusion
  147.6 0.9 copy.22
  148.6 0.7 copy-done.1
  149.8 5.5 %finish.1 = (bf16[4,256,1024]{2,1,0:T(8,128)(2,1)}, f32[4,256,1]{2,1,0:T(8,128)}) custom-call(f32[32,2304]{1,0:T(8,128)} %reduce.2.after_ref, bf16[4,256,1024]{2,1,0:T(8,128)(2,1)} %images_ref.3, f32[4,256,1]{2,1,0:T(8,128)} %copy.15.styles_ref, bf16[1,256,1024]{2,1,0:T(8,128)(2,1)} %get-tuple-element.23.rest_0_, bf16[1,256,1024]{2,1,0:T(8,128)(2,1)} %copy-done.1, ...), custom_call_target="tpu_custom_call" | custom-call | tf_op jit(solution)/shard_map/finish/pallas_call | solution.py:385
  155.3 1.2 reduce.1
  156.6 0.6 add_add_fusion
  (28 shorter events, 2.4 us)
Async XLA Ops:
  2.4 7.1 %copy-start.7 = (f32[4,512]{1,0:T(4,128)S(1)}, f32[4,512]{1,0:T(4,128)}, u32[]{:S(2)}) copy-start(f32[4,512]{1,0:T(4,128)} %param.5) | copy-start | bytes 24580
  2.4 7.2 %copy-start.5 = (bf16[9,256,32]{1,2,0:T(8,128)(2,1)S(1)}, bf16[9,256,32]{1,2,0:T(8,128)(2,1)}, u32[]{:S(2)}) copy-start(bf16[9,256,32]{1,2,0:T(8,128)(2,1)} %param.6) | copy-start | bytes 442372
  6.5 70.6 %collective-permute-start = (bf16[4,256,1024]{2,1,0:T(8,128)(2,1)}, bf16[4,256,1024]{2,1,0:T(8,128)(2,1)}, u32[]{:S(2)}, u32[]{:S(2)}) collective-permute-start(bf16[4,256,1024]{2,1,0:T(8,128)(2,1)} %modulate.1.after_ref.rest_0_), channel_id=1, source_target_pairs={{0,1},{1,0},{2,3},{3,2},{4,5},{5,4},{6,7},{7,6},{8,9},{9,8},{10,11... | collective-permute-start | bytes 6291464 | tf_op jit(solution)/shard_map/ppermute | solution.py:285
  48.6 99.9 %collective-permute-start.1 = (bf16[1,256,1024]{2,1,0:T(8,128)(2,1)}, bf16[1,256,1024]{2,1,0:T(8,128)(2,1)S(1)}, u32[]{:S(2)}, u32[]{:S(2)}) collective-permute-start(bf16[1,256,1024]{2,1,0:T(8,128)(2,1)} %get-tuple-element.24), channel_id=1, source_target_pairs={{0,1},{1,0},{2,3},{3,2},{4,5},{5,4},{6,7},{7,6},{8,9},{9,8},{10,11... | collective-permute-start | bytes 1572872 | tf_op jit(solution)/shard_map/ppermute | solution.py:285
  57.1 91.4 %collective-permute-start.2 = (bf16[1,256,1024]{2,1,0:T(8,128)(2,1)}, bf16[1,256,1024]{2,1,0:T(8,128)(2,1)S(1)}, u32[]{:S(2)}, u32[]{:S(2)}) collective-permute-start(bf16[1,256,1024]{2,1,0:T(8,128)(2,1)} %get-tuple-element.26), channel_id=1, source_target_pairs={{0,1},{1,0},{2,3},{3,2},{4,5},{5,4},{6,7},{7,6},{8,9},{9,8},{10,11... | collective-permute-start | bytes 1572872 | tf_op jit(solution)/shard_map/ppermute | solution.py:285
  66.5 82.0 %collective-permute-start.3 = (bf16[1,256,1024]{2,1,0:T(8,128)(2,1)}, bf16[1,256,1024]{2,1,0:T(8,128)(2,1)S(1)}, u32[]{:S(2)}, u32[]{:S(2)}) collective-permute-start(bf16[1,256,1024]{2,1,0:T(8,128)(2,1)} %get-tuple-element.28), channel_id=1, source_target_pairs={{0,1},{1,0},{2,3},{3,2},{4,5},{5,4},{6,7},{7,6},{8,9},{9,8},{10,11... | collective-permute-start | bytes 1572872 | tf_op jit(solution)/shard_map/ppermute | solution.py:285
  74.9 73.7 %collective-permute-start.4 = (bf16[1,256,1024]{2,1,0:T(8,128)(2,1)}, bf16[1,256,1024]{2,1,0:T(8,128)(2,1)S(1)}, u32[]{:S(2)}, u32[]{:S(2)}) collective-permute-start(bf16[1,256,1024]{2,1,0:T(8,128)(2,1)} %get-tuple-element.30), channel_id=1, source_target_pairs={{0,1},{1,0},{2,3},{3,2},{4,5},{5,4},{6,7},{7,6},{8,9},{9,8},{10,11... | collective-permute-start | bytes 1572872 | tf_op jit(solution)/shard_map/ppermute | solution.py:285
  117.3 28.1 %copy-start = (f32[16,32,256]{2,1,0:T(8,128)S(1)}, f32[16,32,256]{2,1,0:T(8,128)}, u32[]{:S(2)}) copy-start(f32[16,32,256]{2,1,0:T(8,128)} %get-tuple-element.19) | copy-start | bytes 1572868
  117.3 28.1 %copy-start.6 = (f32[256,128]{1,0:T(8,128)S(1)}, f32[256,128]{1,0:T(8,128)}, u32[]{:S(2)}) copy-start(f32[256,128]{1,0:T(8,128)} %get-tuple-element.33) | copy-start | bytes 393220
  146.0 10.6 %collective-permute-start.5 = (bf16[4,256]{1,0:T(4,128)(2,1)S(1)}, bf16[4,256]{1,0:T(4,128)(2,1)S(1)}, u32[]{:S(2)}, u32[]{:S(2)}) collective-permute-start(bf16[4,256]{1,0:T(4,128)(2,1)S(1)} %constant_dynamic-slice_fusion), channel_id=1, source_target_pairs={{0,1},{1,0},{2,3},{3,2},{4,5},{5,4},{6,7},{7,6},{8,9},{9,8},{10,11... | collective-permute-start | bytes 6152 | tf_op jit(solution)/shard_map/ppermute | solution.py:285
  148.5 0.8 copy-start.1
  148.5 1.0 copy-start.2
  148.5 1.1 copy-start.3
  148.6 1.3 copy-start.4

commit v2 on v1

--- a/solution.py
+++ b/solution.py
@@ -9,51 +9,65 @@
 from jax.sharding import PartitionSpec as P
 
 epsilon = 1e-08
-tap_steps = [(-1, -1), (-1, 0), (-1, 1), (0, -1), (0, 0), (0, 1), (1, -1), (1, 0), (1, 1)]
-TAPS = len(tap_steps)
+TAPS = 9
 BF16 = jnp.bfloat16
 F32 = jnp.float32
 HIGHEST = lax.Precision.HIGHEST
 LANES = 128
-ROWS = 32
 VMEM = 56 * 2**20
 MESH = pl.DeviceIdType.MESH
 
 
-def shifted(values, row_step, col_step, side, row, column):
-    pixels = values.shape[1]
-    offset = row_step * side + col_step
-    if offset == 0:
-        return values
-    moved = pltpu.roll(values, (-offset) % pixels, 1)
-    inside = None
-    for step, place in ((row_step, row), (col_step, column)):
-        if step:
-            ok = place >= 1 if step < 0 else place < side - 1
-            inside = ok if inside is None else inside & ok
-    return jnp.where(inside, moved, jnp.zeros_like(moved))
-
-
-def places(rows, pixels, side):
-    pixel = lax.broadcasted_iota(jnp.int32, (rows, pixels), 1)
-    return pixel // side, pixel % side
+def spread(columns, at, lane, stride, values, side):
+    rows, width = values.shape
+    column = lax.broadcasted_iota(jnp.int32, values.shape, 0) % side
+    for group, moved in enumerate(
+        (
+            jnp.where(column >= 1, pltpu.roll(values, 1, 0), 0.0),
+            values,
+            jnp.where(column < side - 1, pltpu.roll(values, rows - 1, 0), 0.0),
+        )
+    ):
+        start = group * stride + lane
+        columns[side + at : side + at + rows, start : start + width] = moved.astype(BF16)
+
+
+def clear_margins(columns, side):
+    margin = jnp.zeros((side, columns.shape[1]), BF16)
+    columns[:side, :] = margin
+    columns[columns.shape[0] - side :, :] = margin
+
+
+def convolve(columns, weights, pixels, side):
+    depth = columns.shape[1]
+    total = 0.0
+    for row in range(3):
+        total = total + jnp.dot(
+            columns[row * side : row * side + pixels, :],
+            weights[row * depth : (row + 1) * depth, :],
+            preferred_element_type=F32,
+        )
+    return total
 
 
 def back_kernel(side, n, me_ref, upstream_ref, factor_ref, weight_ref, *rest):
-    out_refs, columns, terms = rest[:n], rest[n], rest[n + 1]
+    out_refs, columns, turned, terms = rest[:n], rest[n], rest[n + 1], rest[n + 2]
     outputs, pixels = upstream_ref.shape[1:]
     block = weight_ref.shape[0] // n
-    row, column = places(ROWS, pixels, side)
-
-    @pl.loop(0, outputs // ROWS)
-    def _(chunk):
-        rows = pl.ds(pl.multiple_of(chunk * ROWS, ROWS), ROWS)
-        scaled = (upstream_ref[0, rows, :].astype(F32) * factor_ref[0, rows, :]).astype(BF16)
-        for tap, (row_step, col_step) in enumerate(tap_steps):
-            place = pl.ds(pl.multiple_of(tap * outputs + chunk * ROWS, ROWS), ROWS)
-            columns[place, :] = shifted(scaled, -row_step, -col_step, side, row, column).astype(BF16)
-
-    terms[...] = jnp.dot(weight_ref[...], columns[...], preferred_element_type=F32).astype(BF16)
+
+    @pl.when(pl.program_id(0) == 0)
+    def _():
+        clear_margins(columns, side)
+        for tap in range(TAPS):
+            mirror = TAPS - 1 - tap
+            turned[mirror * outputs : (mirror + 1) * outputs, :] = weight_ref[
+                :, tap * outputs : (tap + 1) * outputs
+            ].T
+
+    for at in range(0, pixels, LANES):
+        scaled = upstream_ref[0, :, at : at + LANES].astype(F32) * factor_ref[0]
+        spread(columns, at, 0, outputs, scaled.T, side)
+    terms[...] = convolve(columns, turned, pixels, side).astype(BF16).T
     for step in range(n):
         owner = lax.rem(me_ref[0] + step, n)
         out_refs[step][0] = terms[pl.ds(pl.multiple_of(owner * block, block), block), :]
@@ -61,53 +75,49 @@
 
 def forward_kernel(side, n, me_ref, upstream_ref, factor_ref, squares_ref, weight_ref, *rest):
     maps = rest[:n]
-    output_ref, energy_ref, gradient_ref, columns, scaled_ref, forward_ref, total = rest[n:]
+    output_ref, energy_ref, gradient_ref, columns, forward_ref, radial_ref, total = rest[n:]
     outputs, pixels = upstream_ref.shape[1:]
-    block = maps[0].shape[1]
+    block = maps[0].shape[2]
     inputs = n * block
     image = pl.program_id(0)
-    row, column = places(ROWS, pixels, side)
+
+    def rows_of(step):
+        owner = lax.rem(me_ref[0] + n - step, n)
+        return pl.ds(pl.multiple_of(owner * block, block), block)
 
     @pl.when(image == 0)
     def _():
+        clear_margins(columns, side)
         for tap in range(TAPS):
-            forward_ref[:, tap * inputs : (tap + 1) * inputs] = weight_ref[:, tap * outputs : (tap + 1) * outputs].T
+            for step in range(n):
+                at = tap * inputs + step * block
+                forward_ref[at : at + block, :] = weight_ref[rows_of(step), tap * outputs : (tap + 1) * outputs]
         total[...] = jnp.zeros_like(total)
         energy_ref[...] = jnp.zeros_like(energy_ref)
 
     for step in range(n):
-        owner = lax.rem(me_ref[0] + n - step, n)
-
-        @pl.loop(0, block // ROWS)
-        def _(chunk):
-            rows = pl.ds(pl.multiple_of(chunk * ROWS, ROWS), ROWS)
-            values = maps[step][0, rows, :]
-            for tap, (row_step, col_step) in enumerate(tap_steps):
-                place = pl.ds(pl.multiple_of(tap * inputs + owner * block + chunk * ROWS, ROWS), ROWS)
-                columns[place, :] = shifted(values, row_step, col_step, side, row, column).astype(BF16)
+        for at in range(0, pixels, LANES):
+            spread(columns, at, step * block, inputs, maps[step][0, at : at + LANES, :].astype(F32), side)
 
     factor = factor_ref[0]
+    convolved = convolve(columns, forward_ref, pixels, side).T
+    output_ref[0] = (factor * convolved).astype(BF16)
     upstream = upstream_ref[0].astype(F32)
-    scaled_ref[...] = (upstream * factor).astype(BF16)
-    convolved = jnp.dot(forward_ref[...], columns[...], preferred_element_type=F32)
-    output_ref[0] = (factor * convolved).astype(BF16)
-    norm_grad = jnp.sum(upstream_ref[0].astype(F32) * convolved, axis=1, keepdims=True)
+    norm_grad = jnp.sum(upstream * convolved, axis=1, keepdims=True)
     energy_grad = -0.5 * norm_grad * (factor * factor * factor)
     lane = lax.broadcasted_iota(jnp.int32, energy_ref.shape, 1)
     energy_ref[...] += jnp.where(lane == image, energy_grad, 0.0)
 
-    group = 3 * inputs
-    for at in range(0, TAPS * inputs, group):
-        total[at : at + group, :] += lax.dot_general(
-            columns[at : at + group, :],
-            scaled_ref[...],
-            (((1,), (1,)), ((), ())),
-            preferred_element_type=F32,
+    scaled = (upstream * factor).astype(BF16)
+    depth = 3 * inputs
+    for row in range(3):
+        total[:, row * depth : (row + 1) * depth] += jnp.dot(
+            scaled, columns[row * side : row * side + pixels, :], preferred_element_type=F32
         )
 
     @pl.when(image == pl.num_programs(0) - 1)
     def _():
-        radial = 2.0 * lax.dot_general(
+        radial_ref[...] = 2.0 * lax.dot_general(
             squares_ref[...],
             energy_ref[...],
             (((1,), (1,)), ((), ())),
@@ -116,9 +126,12 @@
         )
         for tap in range(TAPS):
             part = slice(tap * outputs, (tap + 1) * outputs)
-            gradient_ref[:, part] = (
-                total[tap * inputs : (tap + 1) * inputs, :] + weight_ref[:, part].astype(F32) * radial
-            ).astype(BF16)
+            for step in range(n):
+                at = tap * inputs + step * block
+                gradient_ref[rows_of(step), part] = (
+                    total[:, at : at + block].T
+                    + weight_ref[rows_of(step), part].astype(F32) * radial_ref[rows_of(step), :]
+                ).astype(BF16)
 
 
 def flipped(me, distances):
@@ -219,18 +232,17 @@
 
 
 def modulate_kernel(images_ref, styles_ref, modulated_ref):
-    modulated_ref[...] = (images_ref[...].astype(F32) * styles_ref[...]).astype(BF16)
-
-
-def finish_kernel(n, after_ref, images_ref, styles_ref, *rest):
+    modulated_ref[0] = (images_ref[0].astype(F32) * styles_ref[0]).astype(BF16).T
+
+
+def finish_kernel(after_ref, images_ref, styles_ref, *rest):
     del after_ref
     parts, (input_ref, style_ref) = rest[:-2], rest[-2:]
-    for image in range(images_ref.shape[0]):
-        total = 0.0
-        for part in parts[image * n : (image + 1) * n]:
-            total = total + part[0].astype(F32)
-        input_ref[image] = (total * styles_ref[image]).astype(BF16)
-        style_ref[image] = jnp.sum(total * images_ref[image].astype(F32), axis=1, keepdims=True)
+    total = 0.0
+    for part in parts:
+        total = total + part[0].astype(F32)
+    input_ref[0] = (total * styles_ref[0]).astype(BF16)
+    style_ref[0] = jnp.sum(total * images_ref[0].astype(F32), axis=1, keepdims=True)
 
 
 def exchange_scratch(size, parts, rows, buffers):
@@ -291,9 +303,9 @@
     modulated = pl.pallas_call(
         modulate_kernel,
         grid=(batch,),
-        out_shape=jax.ShapeDtypeStruct(images.shape, BF16),
+        out_shape=jax.ShapeDtypeStruct((batch, pixels, block), BF16),
         in_specs=[one_image, pl.BlockSpec((1, block, 1), lambda i: (i, 0, 0))],
-        out_specs=one_image,
+        out_specs=pl.BlockSpec((1, pixels, block), lambda i: (i, 0, 0)),
         compiler_params=plan,
         name="modulate",
     )(images, local_styles[:, :, None])
@@ -311,31 +323,34 @@
 
     smem = pl.BlockSpec(memory_space=pltpu.SMEM)
     work = 2 * TAPS * inputs * outputs * pixels
-    backs = []
-    for image in range(batch):
-        at = functools.partial(lambda image, i: (image, 0, 0), image)
-        parts = pl.pallas_call(
-            functools.partial(back_kernel, side, n),
-            grid=(1,),
-            out_shape=[jax.ShapeDtypeStruct((1, block, pixels), BF16)] * n,
-            in_specs=[
-                smem,
-                pl.BlockSpec((1, outputs, pixels), at),
-                pl.BlockSpec((1, outputs, 1), at),
-                pl.BlockSpec(by_input.shape, lambda i: (0, 0)),
-            ],
-            out_specs=[pl.BlockSpec((1, block, pixels), lambda i: (0, 0, 0))] * n,
-            scratch_shapes=[pltpu.VMEM((TAPS * outputs, pixels), BF16), pltpu.VMEM((inputs, pixels), BF16)],
-            compiler_params=pltpu.CompilerParams(vmem_limit_bytes=VMEM),
-            cost_estimate=pl.CostEstimate(flops=work, bytes_accessed=8 * outputs * pixels, transcendentals=0),
-            name="back",
-        )(position, cotangent, factor, by_input)
-        backs.append([parts[0]] + [send(parts[step], step) for step in range(1, n)])
+    one = lambda i: (i, 0, 0)
+    whole = lambda i: (0, 0)
+    parts = pl.pallas_call(
+        functools.partial(back_kernel, side, n),
+        grid=(batch,),
+        out_shape=[jax.ShapeDtypeStruct((batch, block, pixels), BF16)] * n,
+        in_specs=[
+            smem,
+            pl.BlockSpec((1, outputs, pixels), one),
+            pl.BlockSpec((1, outputs, 1), one),
+            pl.BlockSpec(by_input.shape, whole),
+        ],
+        out_specs=[pl.BlockSpec((1, block, pixels), one)] * n,
+        scratch_shapes=[
+            pltpu.VMEM((pixels + 2 * side, 3 * outputs), BF16),
+            pltpu.VMEM((TAPS * outputs, inputs), BF16),
+            pltpu.VMEM((inputs, pixels), BF16),
+        ],
+        compiler_params=plan,
+        cost_estimate=pl.CostEstimate(
+            flops=batch * work, bytes_accessed=8 * batch * outputs * pixels, transcendentals=0
+        ),
+        name="back",
+    )(position, cotangent, factor, by_input)
+    backs = [send(part, step) if step else part for step, part in enumerate(parts)]
 
     lanes = -(-batch // LANES) * LANES
     squares = jnp.pad(style_square.T, ((0, 0), (0, lanes - batch)))
-    one = lambda i: (i, 0, 0)
-    whole = lambda i: (0, 0)
     output, energy_columns, gradient = pl.pallas_call(
         functools.partial(forward_kernel, side, n),
         grid=(batch,),
@@ -351,17 +366,17 @@
             pl.BlockSpec(squares.shape, whole),
             pl.BlockSpec(by_input.shape, whole),
         ]
-        + [pl.BlockSpec((1, block, pixels), one)] * n,
+        + [pl.BlockSpec((1, pixels, block), one)] * n,
         out_specs=[
             pl.BlockSpec((1, outputs, pixels), one),
             pl.BlockSpec((outputs, lanes), whole),
             pl.BlockSpec((inputs, TAPS * outputs), whole),
         ],
         scratch_shapes=[
-            pltpu.VMEM((TAPS * inputs, pixels), BF16),
-            pltpu.VMEM((outputs, pixels), BF16),
-            pltpu.VMEM((outputs, TAPS * inputs), BF16),
-            pltpu.VMEM((TAPS * inputs, outputs), F32),
+            pltpu.VMEM((pixels + 2 * side, 3 * inputs), BF16),
+            pltpu.VMEM((TAPS * inputs, outputs), BF16),
+            pltpu.VMEM((inputs, outputs), F32),
+            pltpu.VMEM((outputs, TAPS * inputs), F32),
         ],
         compiler_params=pltpu.CompilerParams(vmem_limit_bytes=VMEM),
         cost_estimate=pl.CostEstimate(
@@ -383,16 +398,18 @@
         style_sum = style_sum + (send(part, step) if step else part).astype(F32)
 
     input_grad, style_part = pl.pallas_call(
-        functools.partial(finish_kernel, n),
+        finish_kernel,
+        grid=(batch,),
         out_shape=[
             jax.ShapeDtypeStruct(images.shape, BF16),
             jax.ShapeDtypeStruct((batch, block, 1), F32),
         ],
-        in_specs=[pl.BlockSpec(memory_space=pl.ANY)] + [vmem] * (2 + n * batch),
-        out_specs=[vmem, vmem],
+        in_specs=[pl.BlockSpec(memory_space=pl.ANY), one_image, pl.BlockSpec((1, block, 1), one)]
+        + [one_image] * n,
+        out_specs=[one_image, pl.BlockSpec((1, block, 1), one)],
         compiler_params=plan,
         name="finish",
-    )(gradient, images, local_styles[:, :, None], *[part for parts in backs for part in parts])
+    )(gradient, images, local_styles[:, :, None], *backs)
     style_grad = style_part[:, :, 0] + style_sum
     return (output, input_grad, style_grad, weight_grad)
 

time: 158 us -> 127 us (0.80)
  Pallas kernels: 137 us -> 110 us
  starting transfers between devices: 7.61 us -> 4.16 us
    pallas_call x5 -> x2, Pallas kernels: 37 us -> 22.4 us  [the longest x1 17.1 us: on_device(): pl.pallas_call(functools.partial(back_kernel, side, n), grid=(batch,), ou...]
    pallas_call x1, Pallas kernels: 40.1 us -> 27.5 us  [on_device(): pl.pallas_call(functools.partial(forward_kernel, side, n), grid=(batch,),...]
    ppermute x6 -> x3, starting transfers between devices: 7.61 us -> 4.16 us  [send(): return lax.ppermute(values, 'cout', [(j, (j + step) % n) for j in range(n)])]
  transfers between devices with their start and end apart: 6 -> 3, of which waited for: 0 -> 0; matrix products, arithmetic and copies ran while one was open for 5% -> 6% of each run, Pallas kernels for 85% -> 84%
where the time goes in v2:
time: 127 us
  Pallas kernels  110 us (87%)
  local copies, waits for them, and re-layouts  6.6 us (5%)
  starting transfers between devices  4.16 us (3%)
  other arithmetic  2.86 us (2%)
  matrix products  2.15 us (2%)
    pallas_call x1, Pallas kernels, reduce_rows(): pl.pallas_call(functools.partial(reduce_kernel, size, parts), out_shape=j...  28.2 us
    pallas_call x1, Pallas kernels, gather_rows(): pl.pallas_call(functools.partial(gather_kernel, size, parts, TAPS), out_s...  27.9 us
    pallas_call x1, Pallas kernels, on_device(): pl.pallas_call(functools.partial(forward_kernel, side, n), grid=(batch,),...  27.5 us
    pallas_call x1, Pallas kernels, on_device(): pl.pallas_call(functools.partial(back_kernel, side, n), grid=(batch,), ou...  17.1 us
    pallas_call x1, Pallas kernels, on_device(): pl.pallas_call(finish_kernel, grid=(batch,), out_shape=[jax.ShapeDtypeStr...  5.25 us
    pallas_call x1, Pallas kernels, on_device(): pl.pallas_call(modulate_kernel, grid=(batch,), out_shape=jax.ShapeDtypeSt...  4.38 us
    ppermute x3, starting transfers between devices, send(): return lax.ppermute(values, 'cout', [(j, (j + step) % n) for j in range(n)])  4.16 us
  transfers between devices with their start and end apart: 3, of which 0 were waited for; matrix products, arithmetic and copies ran while one was open for 6% of the time, Pallas kernels for 84%

profile of v2, /device:TPU:0, one launch (start us, length us, event | category | flops | bytes accessed | tf_op | source)
XLA Modules:
  0.0 126.8 jit_solution(9233708249429811978)
XLA Ops:
  0.6 0.7 dynamic-slice_bitcast_fusion
  1.3 1.0 copy.15.styles_ref
  2.3 4.4 %modulate.1.after_ref.rest_0_ = bf16[4,1024,256]{2,1,0:T(8,128)(2,1)} custom-call(bf16[4,256,1024]{2,1,0:T(8,128)(2,1)} %images_ref.3, f32[4,256,1]{2,1,0:T(8,128)} %copy.15.styles_ref), custom_call_target="tpu_custom_call" | custom-call | tf_op jit(solution)/shard_map/modulate/pallas_call | solution.py:303
  6.7 2.9 %collective-permute-start = (bf16[4,1024,256]{2,1,0:T(8,128)(2,1)}, bf16[4,1024,256]{2,1,0:T(8,128)(2,1)}, u32[]{:S(2)}, u32[]{:S(2)}) collective-permute-start(bf16[4,1024,256]{2,1,0:T(8,128)(2,1)} %modulate.1.after_ref.rest_0_), channel_id=1, source_target_pairs={{0,1},{1,0},{2,3},{3,2},{4,5},{5,4},{6,7},{7,6},{8,9},{9,8},{10,11... | collective-permute-start | bytes 6291464 | tf_op jit(solution)/shard_map/ppermute | solution.py:297
  9.7 0.1 copy.12
  9.8 0.7 copy.20
  10.5 27.9 %gather.1 = (bf16[16,32,2304]{2,1,0:T(8,128)(2,1)}, f32[16,32,256]{2,1,0:T(8,128)}) custom-call(bf16[32,2304]{1,0:T(8,128)(2,1)} %bitcast.20, bf16[4,1024,256]{2,1,0:T(8,128)(2,1)} %modulate.1.after_ref.rest_0_), custom_call_target="tpu_custom_call" | custom-call | tf_op jit(solution)/shard_map/gather/pallas_call | solution.py:259
  38.4 1.6 %fusion.2 = f32[4,256,1]{1,0,2:T(4,128)S(1)} fusion(f32[512,256]{1,0:T(8,128)} %bitcast.17, f32[4,512]{0,1:T(8,128)S(1)} %copy.12), kind=kOutput, calls=%fused_computation.4 | convolution fusion | flops 6294528 | bytes 536576 | tf_op jit(solution)/shard_map/dot_general | solution.py:320
  40.0 1.1 copy.16.factor_ref
  41.0 17.1 %back.1 = (bf16[4,256,1024]{2,1,0:T(8,128)(2,1)}, bf16[4,256,1024]{2,1,0:T(8,128)(2,1)}) custom-call(s32[1]{0:T(128)} %bitcast.me_ref, bf16[4,256,1024]{2,1,0:T(8,128)(2,1)} %upstream_ref.3, f32[4,256,1]{2,1,0:T(8,128)} %copy.16.factor_ref, bf16[512,2304]{1,0:T(8,128)(2,1)} %bitcast.22), custom_call_target="tpu_custom_call" | custom-call | flops 9663676416 | bytes 8388608 | tf_op jit(solution)/shard_map/back/pallas_call | solution.py:328
  58.1 0.5 collective-permute-start.1
  58.7 0.7 pad.4.squares_ref
  59.4 0.0 collective-permute-done.rest_1_
  59.4 27.5 %forward.1 = (bf16[4,256,1024]{2,1,0:T(8,128)(2,1)}, f32[256,128]{1,0:T(8,128)}, bf16[512,2304]{1,0:T(8,128)(2,1)}) custom-call(s32[1]{0:T(128)} %bitcast.me_ref, bf16[4,256,1024]{2,1,0:T(8,128)(2,1)} %upstream_ref.3, f32[4,256,1]{2,1,0:T(8,128)} %copy.16.factor_ref, f32[512,128]{1,0:T(8,128)} %pad.4.squares_ref, bf16[512,2304]{1,0:T(8,128)(2,1)} %bitcast.23, ...), custom_call_target="tpu_custom_call" | custom-call | flops 19327352832 | bytes 16777216 | tf_op jit(solution)/shard_map/forward/pallas_call | solution.py:354
  86.9 28.2 %reduce.2.after_ref = f32[32,2304]{1,0:T(8,128)} custom-call(bf16[16,32,2304]{2,1,0:T(8,128)(2,1)} %bitcast.16), custom_call_target="tpu_custom_call" | custom-call | tf_op jit(solution)/shard_map/reduce/pallas_call | solution.py:277
  115.1 0.6 fusion
  115.7 0.7 collective-permute-start.2
  116.4 1.0 broadcast_multiply_fusion
  117.4 0.1 mul.42
  117.4 0.9 copy.19
  118.3 1.3 %copy-done = bf16[4,256,1024]{2,1,0:T(8,128)(2,1)} copy-done((bf16[4,256,1024]{2,1,0:T(8,128)(2,1)}, bf16[4,256,1024]{2,1,0:T(8,128)(2,1)S(1)}, u32[]{:S(2)}) %copy-start) | copy-done | bytes 2097176
  119.7 5.2 %finish.1 = (bf16[4,256,1024]{2,1,0:T(8,128)(2,1)}, f32[4,256,1]{2,1,0:T(8,128)}) custom-call(f32[32,2304]{1,0:T(8,128)} %reduce.2.after_ref, bf16[4,256,1024]{2,1,0:T(8,128)(2,1)} %images_ref.3, f32[4,256,1]{2,1,0:T(8,128)} %copy.15.styles_ref, bf16[4,256,1024]{2,1,0:T(8,128)(2,1)} %get-tuple-element.17.rest_0_, bf16[4,256,1024]{2,1,0:T(8,128)(2,1)} %copy-done), custom_call_target="tpu_custom_call" | custom-call | tf_op jit(solution)/shard_map/finish/pallas_call | solution.py:400
  124.9 1.2 reduce.1
  126.2 0.6 add_add_fusion
  (13 shorter events, 0.0 us)
Async XLA Ops:
  2.3 7.3 %copy-start.4 = (f32[4,512]{1,0:T(4,128)S(1)}, f32[4,512]{1,0:T(4,128)}, u32[]{:S(2)}) copy-start(f32[4,512]{1,0:T(4,128)} %param.5) | copy-start | bytes 24580
  2.3 7.5 %copy-start.2 = (bf16[9,256,32]{1,2,0:T(8,128)(2,1)S(1)}, bf16[9,256,32]{1,2,0:T(8,128)(2,1)}, u32[]{:S(2)}) copy-start(bf16[9,256,32]{1,2,0:T(8,128)(2,1)} %param.6) | copy-start | bytes 442372
  6.7 52.7 %collective-permute-start = (bf16[4,1024,256]{2,1,0:T(8,128)(2,1)}, bf16[4,1024,256]{2,1,0:T(8,128)(2,1)}, u32[]{:S(2)}, u32[]{:S(2)}) collective-permute-start(bf16[4,1024,256]{2,1,0:T(8,128)(2,1)} %modulate.1.after_ref.rest_0_), channel_id=1, source_target_pairs={{0,1},{1,0},{2,3},{3,2},{4,5},{5,4},{6,7},{7,6},{8,9},{9,8},{10,11... | collective-permute-start | bytes 6291464 | tf_op jit(solution)/shard_map/ppermute | solution.py:297
  58.1 60.2 %collective-permute-start.1 = (bf16[4,256,1024]{2,1,0:T(8,128)(2,1)}, bf16[4,256,1024]{2,1,0:T(8,128)(2,1)S(1)}, u32[]{:S(2)}, u32[]{:S(2)}) collective-permute-start(bf16[4,256,1024]{2,1,0:T(8,128)(2,1)} %get-tuple-element.18), channel_id=1, source_target_pairs={{0,1},{1,0},{2,3},{3,2},{4,5},{5,4},{6,7},{7,6},{8,9},{9,8},{10,11... | collective-permute-start | bytes 6291464 | tf_op jit(solution)/shard_map/ppermute | solution.py:297
  86.9 28.2 %copy-start.1 = (f32[16,32,256]{2,1,0:T(8,128)S(1)}, f32[16,32,256]{2,1,0:T(8,128)}, u32[]{:S(2)}) copy-start(f32[16,32,256]{2,1,0:T(8,128)} %get-tuple-element.13) | copy-start | bytes 1572868
  86.9 28.2 %copy-start.3 = (f32[256,128]{1,0:T(8,128)S(1)}, f32[256,128]{1,0:T(8,128)}, u32[]{:S(2)}) copy-start(f32[256,128]{1,0:T(8,128)} %get-tuple-element.21) | copy-start | bytes 393220
  115.7 10.5 %collective-permute-start.2 = (bf16[4,256]{1,0:T(4,128)(2,1)S(1)}, bf16[4,256]{1,0:T(4,128)(2,1)S(1)}, u32[]{:S(2)}, u32[]{:S(2)}) collective-permute-start(bf16[4,256]{1,0:T(4,128)(2,1)S(1)} %constant_dynamic-slice_fusion), channel_id=1, source_target_pairs={{0,1},{1,0},{2,3},{3,2},{4,5},{5,4},{6,7},{7,6},{8,9},{9,8},{10,11... | collective-permute-start | bytes 6152 | tf_op jit(solution)/shard_map/ppermute | solution.py:297
  118.3 1.3 %copy-start = (bf16[4,256,1024]{2,1,0:T(8,128)(2,1)}, bf16[4,256,1024]{2,1,0:T(8,128)(2,1)S(1)}, u32[]{:S(2)}) copy-start(bf16[4,256,1024]{2,1,0:T(8,128)(2,1)S(1)} %collective-permute-done.1.rest_1_) | copy-start | bytes 6291460

commit v3 on v2

--- a/solution.py
+++ b/solution.py
@@ -143,11 +143,11 @@
 
 def orders(size, columns):
     distances = [1 << bit for bit in range(size.bit_length() - 1)][::-1]
-    if columns % (2 * LANES) or size < 8:
+    if columns % (3 * LANES) or size < 8:
         return [(slice(0, columns), distances)]
-    half = columns // 2
+    third = columns // 3
     turned = distances[-2:-1] + distances[:-2] + distances[-1:]
-    return [(slice(0, half), distances), (slice(half, columns), turned)]
+    return [(slice(part * third, (part + 1) * third), (distances, turned, distances)[part]) for part in range(3)]
 
 
 def distances_of(order, slot):
@@ -198,7 +198,7 @@
         energy_ref[slot] = energy
 
 
-def reduce_kernel(size, parts, terms_ref, total_ref, send_sem, recv_sem, *scratch):
+def reduce_kernel(size, parts, scale, terms_ref, total_ref, send_sem, recv_sem, *scratch):
     me = lax.axis_index("dp")
     steps = len(parts[0][1])
     work, came = scratch[: len(parts)], scratch[len(parts) :]
@@ -228,11 +228,11 @@
             copies[part].start()
     for part, (columns, _) in enumerate(parts):
         copies[part].wait()
-        total_ref[:, columns] = work[part][0].astype(F32) + came[part][1].astype(F32)
+        total_ref[:, columns] = (work[part][0].astype(F32) + came[part][1].astype(F32)) * scale
 
 
 def modulate_kernel(images_ref, styles_ref, modulated_ref):
-    modulated_ref[0] = (images_ref[0].astype(F32) * styles_ref[0]).astype(BF16).T
+    modulated_ref[0] = (images_ref[0].T.astype(F32) * styles_ref[0]).astype(BF16)
 
 
 def finish_kernel(after_ref, images_ref, styles_ref, *rest):
@@ -242,7 +242,8 @@
     for part in parts:
         total = total + part[0].astype(F32)
     input_ref[0] = (total * styles_ref[0]).astype(BF16)
-    style_ref[0] = jnp.sum(total * images_ref[0].astype(F32), axis=1, keepdims=True)
+    style = jnp.sum(total * images_ref[0].astype(F32), axis=1, keepdims=True)
+    style_ref[0] = jnp.broadcast_to(style, (style.shape[0], LANES)).T[:1, :]
 
 
 def exchange_scratch(size, parts, rows, buffers):
@@ -270,12 +271,12 @@
     )(mine, after)
 
 
-def reduce_rows(terms, size):
+def reduce_rows(terms, size, scale):
     _, rows, columns = terms.shape
     parts = orders(size, columns)
     vmem = pl.BlockSpec(memory_space=pltpu.VMEM)
     return pl.pallas_call(
-        functools.partial(reduce_kernel, size, parts),
+        functools.partial(reduce_kernel, size, parts, scale),
         out_shape=jax.ShapeDtypeStruct((rows, columns), F32),
         in_specs=[vmem],
         out_specs=vmem,
@@ -304,11 +305,11 @@
         modulate_kernel,
         grid=(batch,),
         out_shape=jax.ShapeDtypeStruct((batch, pixels, block), BF16),
-        in_specs=[one_image, pl.BlockSpec((1, block, 1), lambda i: (i, 0, 0))],
+        in_specs=[one_image, pl.BlockSpec((1, 1, block), lambda i: (i, 0, 0))],
         out_specs=pl.BlockSpec((1, pixels, block), lambda i: (i, 0, 0)),
         compiler_params=plan,
         name="modulate",
-    )(images, local_styles[:, :, None])
+    )(images, local_styles[:, None, :])
     maps = [modulated] + [send(modulated, step) for step in range(1, n)]
 
     mine = weight.transpose(2, 0, 1).reshape(weight.shape[2], TAPS * outputs)
@@ -385,9 +386,9 @@
         name="forward",
     )(position, cotangent, factor, squares, by_input, *maps)
 
-    gradient = reduce_rows(gradient.reshape(size, inputs // size, TAPS * outputs), size)
-    image_count = batch * lax.axis_size("dp")
-    weight_grad = gradient.reshape(-1, TAPS, outputs).transpose(1, 2, 0) * (1.0 / image_count)
+    gradient = gradient.reshape(size, inputs // size, TAPS * outputs)
+    gradient = reduce_rows(gradient, size, 1.0 / (batch * size))
+    weight_grad = gradient.reshape(-1, TAPS, outputs).transpose(1, 2, 0)
 
     energy_grad = energy_columns[:, :batch].T
     style_terms = 2.0 * styles * jnp.dot(energy_grad, kernel_energy.T, precision=HIGHEST)
@@ -402,15 +403,15 @@
         grid=(batch,),
         out_shape=[
             jax.ShapeDtypeStruct(images.shape, BF16),
-            jax.ShapeDtypeStruct((batch, block, 1), F32),
+            jax.ShapeDtypeStruct((batch, 1, block), F32),
         ],
         in_specs=[pl.BlockSpec(memory_space=pl.ANY), one_image, pl.BlockSpec((1, block, 1), one)]
         + [one_image] * n,
-        out_specs=[one_image, pl.BlockSpec((1, block, 1), one)],
+        out_specs=[one_image, pl.BlockSpec((1, 1, block), one)],
         compiler_params=plan,
         name="finish",
     )(gradient, images, local_styles[:, :, None], *backs)
-    style_grad = style_part[:, :, 0] + style_sum
+    style_grad = style_part[:, 0, :] + style_sum
     return (output, input_grad, style_grad, weight_grad)
 
 

time: 127 us -> 123 us (0.969)
  Pallas kernels: 110 us -> 104 us
  local copies, waits for them, and re-layouts: 6.6 us -> 8.17 us
  other arithmetic: 2.86 us -> 1.3 us
    pallas_call x1, Pallas kernels: 28.2 us -> 23.3 us  [reduce_rows(): pl.pallas_call(functools.partial(reduce_kernel, size, parts, scale), out_...]
  transfers between devices with their start and end apart: 3 -> 3, of which waited for: 0 -> 0; matrix products, arithmetic and copies ran while one was open for 6% -> 7% of each run, Pallas kernels for 84% -> 82%
where the time goes in v3:
time: 123 us
  Pallas kernels  104 us (85%)
  local copies, waits for them, and re-layouts  8.17 us (7%)
  starting transfers between devices  5.05 us (4%)
  matrix products  3.03 us (2%)
  other arithmetic  1.3 us (1%)
    pallas_call x1, Pallas kernels, on_device(): pl.pallas_call(functools.partial(forward_kernel, side, n), grid=(batch,),...  27.5 us
    pallas_call x1, Pallas kernels, gather_rows(): pl.pallas_call(functools.partial(gather_kernel, size, parts, TAPS), out_s...  27.1 us
    pallas_call x1, Pallas kernels, reduce_rows(): pl.pallas_call(functools.partial(reduce_kernel, size, parts, scale), out_...  23.3 us
    pallas_call x1, Pallas kernels, on_device(): pl.pallas_call(functools.partial(back_kernel, side, n), grid=(batch,), ou...  17.1 us
    pallas_call x1, Pallas kernels, on_device(): pl.pallas_call(finish_kernel, grid=(batch,), out_shape=[jax.ShapeDtypeStr...  5.13 us
    ppermute x3, starting transfers between devices, send(): return lax.ppermute(values, 'cout', [(j, (j + step) % n) for j in range(n)])  5.05 us
    pallas_call x1, Pallas kernels, on_device(): pl.pallas_call(modulate_kernel, grid=(batch,), out_shape=jax.ShapeDtypeSt...  4.17 us
  transfers between devices with their start and end apart: 3, of which 0 were waited for; matrix products, arithmetic and copies ran while one was open for 7% of the time, Pallas kernels for 82%

profile of v3, /device:TPU:0, one launch (start us, length us, event | category | flops | bytes accessed | tf_op | source)
XLA Modules:
  0.0 122.6 jit_solution(16262334509928081793)
XLA Ops:
  0.6 0.7 constant_dynamic-slice_fusion.1
  1.3 0.6 broadcast_in_dim.9.styles_ref
  1.9 4.2 %modulate.1.after_ref.rest_0_ = bf16[4,1024,256]{2,1,0:T(8,128)(2,1)} custom-call(bf16[4,256,1024]{2,1,0:T(8,128)(2,1)} %images_ref.3, f32[4,1,256]{2,1,0:T(1,128)} %broadcast_in_dim.9.styles_ref), custom_call_target="tpu_custom_call" | custom-call | tf_op jit(solution)/shard_map/modulate/pallas_call | solution.py:304
  6.1 2.9 %collective-permute-start = (bf16[4,1024,256]{2,1,0:T(8,128)(2,1)}, bf16[4,1024,256]{2,1,0:T(8,128)(2,1)}, u32[]{:S(2)}, u32[]{:S(2)}) collective-permute-start(bf16[4,1024,256]{2,1,0:T(8,128)(2,1)} %modulate.1.after_ref.rest_0_), channel_id=1, source_target_pairs={{0,1},{1,0},{2,3},{3,2},{4,5},{5,4},{6,7},{7,6},{8,9},{9,8},{10,11... | collective-permute-start | bytes 6291464 | tf_op jit(solution)/shard_map/ppermute | solution.py:298
  9.0 0.1 copy.12
  9.2 0.7 copy.20
  9.9 27.1 %gather.1 = (bf16[16,32,2304]{2,1,0:T(8,128)(2,1)}, f32[16,32,256]{2,1,0:T(8,128)}) custom-call(bf16[32,2304]{1,0:T(8,128)(2,1)} %bitcast.22, bf16[4,1024,256]{2,1,0:T(8,128)(2,1)} %modulate.1.after_ref.rest_0_), custom_call_target="tpu_custom_call" | custom-call | tf_op jit(solution)/shard_map/gather/pallas_call | solution.py:260
  37.0 1.6 %fusion.2 = f32[4,256,1]{1,0,2:T(4,128)S(1)} fusion(f32[512,256]{1,0:T(8,128)} %bitcast.19, f32[4,512]{0,1:T(8,128)S(1)} %copy.12), kind=kOutput, calls=%fused_computation.4 | convolution fusion | flops 6294528 | bytes 536576 | tf_op jit(solution)/shard_map/dot_general | solution.py:321
  38.6 1.0 copy.15.factor_ref
  39.6 17.1 %back.1 = (bf16[4,256,1024]{2,1,0:T(8,128)(2,1)}, bf16[4,256,1024]{2,1,0:T(8,128)(2,1)}) custom-call(s32[1]{0:T(128)} %bitcast.me_ref, bf16[4,256,1024]{2,1,0:T(8,128)(2,1)} %upstream_ref.3, f32[4,256,1]{2,1,0:T(8,128)} %copy.15.factor_ref, bf16[512,2304]{1,0:T(8,128)(2,1)} %bitcast.24), custom_call_target="tpu_custom_call" | custom-call | flops 9663676416 | bytes 8388608 | tf_op jit(solution)/shard_map/back/pallas_call | solution.py:329
  56.7 0.6 collective-permute-start.1
  57.3 0.7 pad.4.squares_ref
  58.0 27.5 %forward.1 = (bf16[4,256,1024]{2,1,0:T(8,128)(2,1)}, f32[256,128]{1,0:T(8,128)}, bf16[512,2304]{1,0:T(8,128)(2,1)}) custom-call(s32[1]{0:T(128)} %bitcast.me_ref, bf16[4,256,1024]{2,1,0:T(8,128)(2,1)} %upstream_ref.3, f32[4,256,1]{2,1,0:T(8,128)} %copy.15.factor_ref, f32[512,128]{1,0:T(8,128)} %pad.4.squares_ref, bf16[512,2304]{1,0:T(8,128)(2,1)} %bitcast.25, ...), custom_call_target="tpu_custom_call" | custom-call | flops 19327352832 | bytes 16777216 | tf_op jit(solution)/shard_map/forward/pallas_call | solution.py:355
  85.5 1.4 %fusion = bf16[4,512]{1,0:T(4,128)(2,1)S(1)} fusion(f32[512,256]{1,0:T(8,128)S(1)} %bitcast.20, f32[256,128]{1,0:T(8,128)} %get-tuple-element.21, f32[4,512]{1,0:T(4,128)S(1)} %copy-done.3), kind=kOutput, calls=%fused_computation.1 | convolution fusion | flops 6297600 | bytes 667648 | tf_op jit(solution)/shard_map/dot_general | solution.py:394
  87.0 1.6 %collective-permute-start.2 = (bf16[4,256]{1,0:T(4,128)(2,1)S(1)}, bf16[4,256]{1,0:T(4,128)(2,1)S(1)}, u32[]{:S(2)}, u32[]{:S(2)}) collective-permute-start(bf16[4,256]{1,0:T(4,128)(2,1)S(1)} %constant_dynamic-slice_fusion), channel_id=1, source_target_pairs={{0,1},{1,0},{2,3},{3,2},{4,5},{5,4},{6,7},{7,6},{8,9},{9,8},{10,11... | collective-permute-start | bytes 6152 | tf_op jit(solution)/shard_map/ppermute | solution.py:298
  88.6 1.0 copy.17.styles_ref
  89.6 23.3 %reduce.1.after_ref = f32[32,2304]{1,0:T(8,128)} custom-call(bf16[16,32,2304]{2,1,0:T(8,128)(2,1)} %bitcast.18), custom_call_target="tpu_custom_call" | custom-call | tf_op jit(solution)/shard_map/reduce/pallas_call | solution.py:278
  112.9 1.0 reshape.31
  113.9 0.9 copy.18
  114.8 0.0 collective-permute-done.1.rest_1_
  114.8 1.3 %copy-done = bf16[4,256,1024]{2,1,0:T(8,128)(2,1)} copy-done((bf16[4,256,1024]{2,1,0:T(8,128)(2,1)}, bf16[4,256,1024]{2,1,0:T(8,128)(2,1)S(1)}, u32[]{:S(2)}) %copy-start) | copy-done | bytes 2097176
  116.2 5.1 %finish.1 = (bf16[4,256,1024]{2,1,0:T(8,128)(2,1)}, f32[4,1,256]{2,1,0:T(1,128)}) custom-call(f32[32,2304]{1,0:T(8,128)} %reduce.1.after_ref, bf16[4,256,1024]{2,1,0:T(8,128)(2,1)} %images_ref.3, f32[4,256,1]{2,1,0:T(8,128)} %copy.17.styles_ref, bf16[4,256,1024]{2,1,0:T(8,128)(2,1)} %get-tuple-element.17.rest_0_, bf16[4,256,1024]{2,1,0:T(8,128)(2,1)} %copy-done), custom_call_target="tpu_custom_call" | custom-call | tf_op jit(solution)/shard_map/finish/pallas_call | solution.py:401
  121.3 0.0 collective-permute-done.2
  121.3 1.3 %bitcast_add_fusion = f32[4,256]{1,0:T(4,128)} fusion(f32[4,1,256]{2,1,0:T(1,128)} %get-tuple-element.20, bf16[4,256]{1,0:T(4,128)(2,1)S(1)} %collective-permute-done.2, bf16[4,512]{1,0:T(4,128)(2,1)S(1)} %fusion, s32[]{:T(128)S(6)} %select_n.10), kind=kLoop, calls=%fused_computation.8 | loop fusion | flops 4096 | bytes 12292 | tf_op jit(solution)/shard_map/add | solution.py:414
  (11 shorter events, 0.0 us)
Async XLA Ops:
  1.9 7.1 %copy-start.3 = (f32[4,512]{1,0:T(4,128)S(1)}, f32[4,512]{1,0:T(4,128)}, u32[]{:S(2)}) copy-start(f32[4,512]{1,0:T(4,128)} %param.5) | copy-start | bytes 24580
  1.9 7.3 %copy-start.2 = (bf16[9,256,32]{1,2,0:T(8,128)(2,1)S(1)}, bf16[9,256,32]{1,2,0:T(8,128)(2,1)}, u32[]{:S(2)}) copy-start(bf16[9,256,32]{1,2,0:T(8,128)(2,1)} %param.6) | copy-start | bytes 442372
  6.1 51.9 %collective-permute-start = (bf16[4,1024,256]{2,1,0:T(8,128)(2,1)}, bf16[4,1024,256]{2,1,0:T(8,128)(2,1)}, u32[]{:S(2)}, u32[]{:S(2)}) collective-permute-start(bf16[4,1024,256]{2,1,0:T(8,128)(2,1)} %modulate.1.after_ref.rest_0_), channel_id=1, source_target_pairs={{0,1},{1,0},{2,3},{3,2},{4,5},{5,4},{6,7},{7,6},{8,9},{9,8},{10,11... | collective-permute-start | bytes 6291464 | tf_op jit(solution)/shard_map/ppermute | solution.py:298
  56.7 58.1 %collective-permute-start.1 = (bf16[4,256,1024]{2,1,0:T(8,128)(2,1)}, bf16[4,256,1024]{2,1,0:T(8,128)(2,1)S(1)}, u32[]{:S(2)}, u32[]{:S(2)}) collective-permute-start(bf16[4,256,1024]{2,1,0:T(8,128)(2,1)} %get-tuple-element.18), channel_id=1, source_target_pairs={{0,1},{1,0},{2,3},{3,2},{4,5},{5,4},{6,7},{7,6},{8,9},{9,8},{10,11... | collective-permute-start | bytes 6291464 | tf_op jit(solution)/shard_map/ppermute | solution.py:298
  58.0 27.5 %copy-start.1 = (f32[16,32,256]{2,1,0:T(8,128)S(1)}, f32[16,32,256]{2,1,0:T(8,128)}, u32[]{:S(2)}) copy-start(f32[16,32,256]{2,1,0:T(8,128)} %get-tuple-element.13) | copy-start | bytes 1572868
  87.0 34.3 %collective-permute-start.2 = (bf16[4,256]{1,0:T(4,128)(2,1)S(1)}, bf16[4,256]{1,0:T(4,128)(2,1)S(1)}, u32[]{:S(2)}, u32[]{:S(2)}) collective-permute-start(bf16[4,256]{1,0:T(4,128)(2,1)S(1)} %constant_dynamic-slice_fusion), channel_id=1, source_target_pairs={{0,1},{1,0},{2,3},{3,2},{4,5},{5,4},{6,7},{7,6},{8,9},{9,8},{10,11... | collective-permute-start | bytes 6152 | tf_op jit(solution)/shard_map/ppermute | solution.py:298
  114.8 1.3 %copy-start = (bf16[4,256,1024]{2,1,0:T(8,128)(2,1)}, bf16[4,256,1024]{2,1,0:T(8,128)(2,1)S(1)}, u32[]{:S(2)}) copy-start(bf16[4,256,1024]{2,1,0:T(8,128)(2,1)S(1)} %collective-permute-done.1.rest_1_) | copy-start | bytes 6291460

commit v4 on v3

--- a/solution.py
+++ b/solution.py
@@ -143,15 +143,23 @@
 
 def orders(size, columns):
     distances = [1 << bit for bit in range(size.bit_length() - 1)][::-1]
-    if columns % (3 * LANES) or size < 8:
+    if columns % (TAPS * LANES) or size < 8:
         return [(slice(0, columns), distances)]
-    third = columns // 3
+    width = columns // TAPS
     turned = distances[-2:-1] + distances[:-2] + distances[-1:]
-    return [(slice(part * third, (part + 1) * third), (distances, turned, distances)[part]) for part in range(3)]
+    return [
+        (slice(part * width, (part + 1) * width), (distances, turned, distances)[part % 3]) for part in range(TAPS)
+    ]
 
 
 def distances_of(order, slot):
     return [distance for bit, distance in enumerate(order) if (slot >> bit) & 1]
+
+
+def taps_in(columns, outputs):
+    first = columns.start // outputs
+    count = (columns.stop - columns.start) // outputs
+    return [(first + tap, tap * outputs, (tap + 1) * outputs) for tap in range(count)]
 
 
 def greet(me, order):
@@ -166,7 +174,8 @@
     del after_ref
     steps = len(parts[0][1])
     for part, (columns, _) in enumerate(parts):
-        held[part][0] = mine_ref[:, columns]
+        for tap, start, stop in taps_in(columns, mine_ref.shape[2]):
+            held[part][0, :, start:stop] = mine_ref[tap]
     greet(me, parts[0][1])
     copies = [None] * len(parts)
     for step in range(steps):
@@ -228,7 +237,9 @@
             copies[part].start()
     for part, (columns, _) in enumerate(parts):
         copies[part].wait()
-        total_ref[:, columns] = (work[part][0].astype(F32) + came[part][1].astype(F32)) * scale
+        total = (work[part][0].astype(F32) + came[part][1].astype(F32)) * scale
+        for tap, start, stop in taps_in(columns, total_ref.shape[2]):
+            total_ref[tap] = total[:, start:stop]
 
 
 def modulate_kernel(images_ref, styles_ref, modulated_ref):
@@ -241,7 +252,8 @@
     total = 0.0
     for part in parts:
         total = total + part[0].astype(F32)
-    input_ref[0] = (total * styles_ref[0]).astype(BF16)
+    styles = jnp.broadcast_to(styles_ref[0], (LANES, styles_ref.shape[2])).T[:, :1]
+    input_ref[0] = (total * styles).astype(BF16)
     style = jnp.sum(total * images_ref[0].astype(F32), axis=1, keepdims=True)
     style_ref[0] = jnp.broadcast_to(style, (style.shape[0], LANES)).T[:1, :]
 
@@ -254,7 +266,8 @@
 
 
 def gather_rows(mine, after, size):
-    rows, columns = mine.shape
+    taps, rows, outputs = mine.shape
+    columns = taps * outputs
     parts = orders(size, columns)
     vmem = pl.BlockSpec(memory_space=pltpu.VMEM)
     return pl.pallas_call(
@@ -277,7 +290,7 @@
     vmem = pl.BlockSpec(memory_space=pltpu.VMEM)
     return pl.pallas_call(
         functools.partial(reduce_kernel, size, parts, scale),
-        out_shape=jax.ShapeDtypeStruct((rows, columns), F32),
+        out_shape=jax.ShapeDtypeStruct((TAPS, rows, columns // TAPS), F32),
         in_specs=[vmem],
         out_specs=vmem,
         scratch_shapes=exchange_scratch(size, parts, rows, 2),
@@ -312,7 +325,7 @@
     )(images, local_styles[:, None, :])
     maps = [modulated] + [send(modulated, step) for step in range(1, n)]
 
-    mine = weight.transpose(2, 0, 1).reshape(weight.shape[2], TAPS * outputs)
+    mine = weight.transpose(0, 2, 1)
     size = lax.axis_size("dp")
     by_input, kernel_energy = gather_rows(mine, modulated, size)
     by_input = by_input.reshape(inputs, TAPS * outputs)
@@ -388,7 +401,7 @@
 
     gradient = gradient.reshape(size, inputs // size, TAPS * outputs)
     gradient = reduce_rows(gradient, size, 1.0 / (batch * size))
-    weight_grad = gradient.reshape(-1, TAPS, outputs).transpose(1, 2, 0)
+    weight_grad = gradient.transpose(0, 2, 1)
 
     energy_grad = energy_columns[:, :batch].T
     style_terms = 2.0 * styles * jnp.dot(energy_grad, kernel_energy.T, precision=HIGHEST)
@@ -405,12 +418,12 @@
             jax.ShapeDtypeStruct(images.shape, BF16),
             jax.ShapeDtypeStruct((batch, 1, block), F32),
         ],
-        in_specs=[pl.BlockSpec(memory_space=pl.ANY), one_image, pl.BlockSpec((1, block, 1), one)]
+        in_specs=[pl.BlockSpec(memory_space=pl.ANY), one_image, pl.BlockSpec((1, 1, block), one)]
         + [one_image] * n,
         out_specs=[one_image, pl.BlockSpec((1, 1, block), one)],
         compiler_params=plan,
         name="finish",
-    )(gradient, images, local_styles[:, :, None], *backs)
+    )(gradient, images, local_styles[:, None, :], *backs)
     style_grad = style_part[:, 0, :] + style_sum
     return (output, input_grad, style_grad, weight_grad)
 

time: 123 us -> 120 us (0.976)
  local copies, waits for them, and re-layouts: 8.17 us -> 5.26 us
    pallas_call x1, Pallas kernels: 23.3 us -> 25.7 us  [reduce_rows(): pl.pallas_call(functools.partial(reduce_kernel, size, parts, scale), out_...]
    pallas_call x1, Pallas kernels: 27.1 us -> 25.1 us  [gather_rows(): pl.pallas_call(functools.partial(gather_kernel, size, parts, TAPS), out_s...]
    reshape x2 -> x0, local copies, waits for them, and re-layouts: 1.69 us -> none  [the longest x1 1.01 us: on_device(): weight_grad = gradient.reshape(-1, TAPS, outputs).transpose(1, 2, 0)]
  transfers between devices with their start and end apart: 3 -> 3, of which waited for: 0 -> 0; matrix products, arithmetic and copies ran while one was open for 7% -> 4% of each run, Pallas kernels for 82% -> 84%
where the time goes in v4:
time: 120 us
  Pallas kernels  105 us (88%)
  local copies, waits for them, and re-layouts  5.26 us (4%)
  starting transfers between devices  5.03 us (4%)
  matrix products  3.03 us (3%)
  other arithmetic  1.31 us (1%)
    pallas_call x1, Pallas kernels, on_device(): pl.pallas_call(functools.partial(forward_kernel, side, n), grid=(batch,),...  27.5 us
    pallas_call x1, Pallas kernels, reduce_rows(): pl.pallas_call(functools.partial(reduce_kernel, size, parts, scale), out_...  25.7 us
    pallas_call x1, Pallas kernels, gather_rows(): pl.pallas_call(functools.partial(gather_kernel, size, parts, TAPS), out_s...  25.1 us
    pallas_call x1, Pallas kernels, on_device(): pl.pallas_call(functools.partial(back_kernel, side, n), grid=(batch,), ou...  17.1 us
    pallas_call x1, Pallas kernels, on_device(): pl.pallas_call(finish_kernel, grid=(batch,), out_shape=[jax.ShapeDtypeStr...  5.13 us
    ppermute x3, starting transfers between devices, send(): return lax.ppermute(values, 'cout', [(j, (j + step) % n) for j in range(n)])  5.03 us
    pallas_call x1, Pallas kernels, on_device(): pl.pallas_call(modulate_kernel, grid=(batch,), out_shape=jax.ShapeDtypeSt...  4.11 us
  transfers between devices with their start and end apart: 3, of which 0 were waited for; matrix products, arithmetic and copies ran while one was open for 4% of the time, Pallas kernels for 84%

profile of v4, /device:TPU:0, one launch (start us, length us, event | category | flops | bytes accessed | tf_op | source)
XLA Modules:
  0.0 120.0 jit_solution(12676553944976246280)
XLA Ops:
  0.6 0.7 constant_dynamic-slice_fusion.1
  1.3 0.6 broadcast_in_dim.7.styles_ref
  1.9 4.1 %modulate.1.after_ref.rest_0_ = bf16[4,1024,256]{2,1,0:T(8,128)(2,1)} custom-call(bf16[4,256,1024]{2,1,0:T(8,128)(2,1)} %images_ref.3, f32[4,1,256]{2,1,0:T(1,128)} %broadcast_in_dim.7.styles_ref), custom_call_target="tpu_custom_call" | custom-call | tf_op jit(solution)/shard_map/modulate/pallas_call | solution.py:317
  6.0 2.9 %collective-permute-start = (bf16[4,1024,256]{2,1,0:T(8,128)(2,1)}, bf16[4,1024,256]{2,1,0:T(8,128)(2,1)}, u32[]{:S(2)}, u32[]{:S(2)}) collective-permute-start(bf16[4,1024,256]{2,1,0:T(8,128)(2,1)} %modulate.1.after_ref.rest_0_), channel_id=1, source_target_pairs={{0,1},{1,0},{2,3},{3,2},{4,5},{5,4},{6,7},{7,6},{8,9},{9,8},{10,11... | collective-permute-start | bytes 6291464 | tf_op jit(solution)/shard_map/ppermute | solution.py:311
  9.0 0.0 copy-done.3
  9.0 0.1 copy.10
  9.1 25.1 %gather.1 = (bf16[16,32,2304]{2,1,0:T(8,128)(2,1)}, f32[16,32,256]{2,1,0:T(8,128)}) custom-call(bf16[9,32,256]{2,1,0:T(8,128)(2,1)} %bitcast.18, bf16[4,1024,256]{2,1,0:T(8,128)(2,1)} %modulate.1.after_ref.rest_0_), custom_call_target="tpu_custom_call" | custom-call | tf_op jit(solution)/shard_map/gather/pallas_call | solution.py:273
  34.2 1.6 %fusion.2 = f32[4,256,1]{1,0,2:T(4,128)S(1)} fusion(f32[512,256]{1,0:T(8,128)} %bitcast.16, f32[4,512]{0,1:T(8,128)S(1)} %copy.10), kind=kOutput, calls=%fused_computation.4 | convolution fusion | flops 6294528 | bytes 536576 | tf_op jit(solution)/shard_map/dot_general | solution.py:334
  35.8 1.0 copy.12.factor_ref
  36.9 17.1 %back.1 = (bf16[4,256,1024]{2,1,0:T(8,128)(2,1)}, bf16[4,256,1024]{2,1,0:T(8,128)(2,1)}) custom-call(s32[1]{0:T(128)} %bitcast.me_ref, bf16[4,256,1024]{2,1,0:T(8,128)(2,1)} %upstream_ref.3, f32[4,256,1]{2,1,0:T(8,128)} %copy.12.factor_ref, bf16[512,2304]{1,0:T(8,128)(2,1)} %bitcast.19), custom_call_target="tpu_custom_call" | custom-call | flops 9663676416 | bytes 8388608 | tf_op jit(solution)/shard_map/back/pallas_call | solution.py:342
  54.0 0.6 collective-permute-start.1
  54.5 0.7 pad.4.squares_ref
  55.3 0.0 collective-permute-done.rest_1_
  55.3 27.5 %forward.1 = (bf16[4,256,1024]{2,1,0:T(8,128)(2,1)}, f32[256,128]{1,0:T(8,128)}, bf16[512,2304]{1,0:T(8,128)(2,1)}) custom-call(s32[1]{0:T(128)} %bitcast.me_ref, bf16[4,256,1024]{2,1,0:T(8,128)(2,1)} %upstream_ref.3, f32[4,256,1]{2,1,0:T(8,128)} %copy.12.factor_ref, f32[512,128]{1,0:T(8,128)} %pad.4.squares_ref, bf16[512,2304]{1,0:T(8,128)(2,1)} %bitcast.20, ...), custom_call_target="tpu_custom_call" | custom-call | flops 19327352832 | bytes 16777216 | tf_op jit(solution)/shard_map/forward/pallas_call | solution.py:368
  82.8 0.0 copy-done.1
  82.8 1.4 %fusion = bf16[4,512]{1,0:T(4,128)(2,1)S(1)} fusion(f32[512,256]{1,0:T(8,128)S(1)} %bitcast.17, f32[256,128]{1,0:T(8,128)} %get-tuple-element.21, f32[4,512]{1,0:T(4,128)S(1)} %copy-done.3), kind=kOutput, calls=%fused_computation.1 | convolution fusion | flops 6297600 | bytes 667648 | tf_op jit(solution)/shard_map/dot_general | solution.py:407
  84.3 1.5 %collective-permute-start.2 = (bf16[4,256]{1,0:T(4,128)(2,1)S(1)}, bf16[4,256]{1,0:T(4,128)(2,1)S(1)}, u32[]{:S(2)}, u32[]{:S(2)}) collective-permute-start(bf16[4,256]{1,0:T(4,128)(2,1)S(1)} %constant_dynamic-slice_fusion), channel_id=1, source_target_pairs={{0,1},{1,0},{2,3},{3,2},{4,5},{5,4},{6,7},{7,6},{8,9},{9,8},{10,11... | collective-permute-start | bytes 6152 | tf_op jit(solution)/shard_map/ppermute | solution.py:311
  85.8 25.7 %reduce.1.after_ref = f32[9,32,256]{2,1,0:T(8,128)} custom-call(bf16[16,32,2304]{2,1,0:T(8,128)(2,1)} %bitcast.15), custom_call_target="tpu_custom_call" | custom-call | tf_op jit(solution)/shard_map/reduce/pallas_call | solution.py:291
  111.5 0.0 collective-permute-done.1.rest_1_
  111.5 1.3 %copy-done.2 = bf16[4,256,1024]{2,1,0:T(8,128)(2,1)} copy-done((bf16[4,256,1024]{2,1,0:T(8,128)(2,1)}, bf16[4,256,1024]{2,1,0:T(8,128)(2,1)S(1)}, u32[]{:S(2)}) %copy-start.2) | copy-done | bytes 2097176
  112.8 5.1 %finish.1 = (bf16[4,256,1024]{2,1,0:T(8,128)(2,1)}, f32[4,1,256]{2,1,0:T(1,128)}) custom-call(f32[9,32,256]{2,1,0:T(8,128)} %reduce.1.after_ref, bf16[4,256,1024]{2,1,0:T(8,128)(2,1)} %images_ref.3, f32[4,1,256]{2,1,0:T(1,128)} %broadcast_in_dim.7.styles_ref, bf16[4,256,1024]{2,1,0:T(8,128)(2,1)} %get-tuple-element.17.rest_0_, bf16[4,256,1024]{2,1,0:T(8,128)(2,1)} %copy-done.2), custom_call_target="tpu_custom_call" | custom-call | tf_op jit(solution)/shard_map/finish/pallas_call | solution.py:414
  118.0 0.0 collective-permute-done.2
  118.0 1.3 %bitcast_add_fusion = f32[4,256]{1,0:T(4,128)} fusion(f32[4,1,256]{2,1,0:T(1,128)} %get-tuple-element.20, bf16[4,256]{1,0:T(4,128)(2,1)S(1)} %collective-permute-done.2, bf16[4,512]{1,0:T(4,128)(2,1)S(1)} %fusion, s32[]{:T(128)S(6)} %select_n.10), kind=kLoop, calls=%fused_computation.8 | loop fusion | flops 4096 | bytes 12292 | tf_op jit(solution)/shard_map/add | solution.py:427
  119.3 0.7 copy.17
  (7 shorter events, 0.0 us)
Async XLA Ops:
  1.9 7.1 %copy-start.3 = (f32[4,512]{1,0:T(4,128)S(1)}, f32[4,512]{1,0:T(4,128)}, u32[]{:S(2)}) copy-start(f32[4,512]{1,0:T(4,128)} %param.5) | copy-start | bytes 24580
  6.0 49.2 %collective-permute-start = (bf16[4,1024,256]{2,1,0:T(8,128)(2,1)}, bf16[4,1024,256]{2,1,0:T(8,128)(2,1)}, u32[]{:S(2)}, u32[]{:S(2)}) collective-permute-start(bf16[4,1024,256]{2,1,0:T(8,128)(2,1)} %modulate.1.after_ref.rest_0_), channel_id=1, source_target_pairs={{0,1},{1,0},{2,3},{3,2},{4,5},{5,4},{6,7},{7,6},{8,9},{9,8},{10,11... | collective-permute-start | bytes 6291464 | tf_op jit(solution)/shard_map/ppermute | solution.py:311
  54.0 57.5 %collective-permute-start.1 = (bf16[4,256,1024]{2,1,0:T(8,128)(2,1)}, bf16[4,256,1024]{2,1,0:T(8,128)(2,1)S(1)}, u32[]{:S(2)}, u32[]{:S(2)}) collective-permute-start(bf16[4,256,1024]{2,1,0:T(8,128)(2,1)} %get-tuple-element.18), channel_id=1, source_target_pairs={{0,1},{1,0},{2,3},{3,2},{4,5},{5,4},{6,7},{7,6},{8,9},{9,8},{10,11... | collective-permute-start | bytes 6291464 | tf_op jit(solution)/shard_map/ppermute | solution.py:311
  55.3 27.5 %copy-start.1 = (f32[16,32,256]{2,1,0:T(8,128)S(1)}, f32[16,32,256]{2,1,0:T(8,128)}, u32[]{:S(2)}) copy-start(f32[16,32,256]{2,1,0:T(8,128)} %get-tuple-element.13) | copy-start | bytes 1572868
  84.3 33.7 %collective-permute-start.2 = (bf16[4,256]{1,0:T(4,128)(2,1)S(1)}, bf16[4,256]{1,0:T(4,128)(2,1)S(1)}, u32[]{:S(2)}, u32[]{:S(2)}) collective-permute-start(bf16[4,256]{1,0:T(4,128)(2,1)S(1)} %constant_dynamic-slice_fusion), channel_id=1, source_target_pairs={{0,1},{1,0},{2,3},{3,2},{4,5},{5,4},{6,7},{7,6},{8,9},{9,8},{10,11... | collective-permute-start | bytes 6152 | tf_op jit(solution)/shard_map/ppermute | solution.py:311
  111.5 1.3 %copy-start.2 = (bf16[4,256,1024]{2,1,0:T(8,128)(2,1)}, bf16[4,256,1024]{2,1,0:T(8,128)(2,1)S(1)}, u32[]{:S(2)}) copy-start(bf16[4,256,1024]{2,1,0:T(8,128)(2,1)S(1)} %collective-permute-done.1.rest_1_) | copy-start | bytes 6291460
  112.8 6.4 %copy-start = (f32[9,32,256]{2,1,0:T(8,128)S(1)}, f32[9,32,256]{2,1,0:T(8,128)}, u32[]{:S(2)}) copy-start(f32[9,32,256]{2,1,0:T(8,128)} %reduce.1.after_ref) | copy-start | bytes 884740

commit v5 on v4

--- a/solution.py
+++ b/solution.py
@@ -32,6 +32,10 @@
         columns[side + at : side + at + rows, start : start + width] = moved.astype(BF16)
 
 
+def as_column(row):
+    return jnp.broadcast_to(row, (LANES, row.shape[1])).T[:, :1]
+
+
 def clear_margins(columns, side):
     margin = jnp.zeros((side, columns.shape[1]), BF16)
     columns[:side, :] = margin
@@ -64,8 +68,9 @@
                 :, tap * outputs : (tap + 1) * outputs
             ].T
 
+    factor = as_column(factor_ref[0])
     for at in range(0, pixels, LANES):
-        scaled = upstream_ref[0, :, at : at + LANES].astype(F32) * factor_ref[0]
+        scaled = upstream_ref[0, :, at : at + LANES].astype(F32) * factor
         spread(columns, at, 0, outputs, scaled.T, side)
     terms[...] = convolve(columns, turned, pixels, side).astype(BF16).T
     for step in range(n):
@@ -99,7 +104,7 @@
         for at in range(0, pixels, LANES):
             spread(columns, at, step * block, inputs, maps[step][0, at : at + LANES, :].astype(F32), side)
 
-    factor = factor_ref[0]
+    factor = as_column(factor_ref[0])
     convolved = convolve(columns, forward_ref, pixels, side).T
     output_ref[0] = (factor * convolved).astype(BF16)
     upstream = upstream_ref[0].astype(F32)
@@ -252,7 +257,7 @@
     total = 0.0
     for part in parts:
         total = total + part[0].astype(F32)
-    styles = jnp.broadcast_to(styles_ref[0], (LANES, styles_ref.shape[2])).T[:, :1]
+    styles = as_column(styles_ref[0])
     input_ref[0] = (total * styles).astype(BF16)
     style = jnp.sum(total * images_ref[0].astype(F32), axis=1, keepdims=True)
     style_ref[0] = jnp.broadcast_to(style, (style.shape[0], LANES)).T[:1, :]
@@ -333,7 +338,7 @@
     style_square = styles * styles
     energy = jnp.dot(style_square, kernel_energy, precision=HIGHEST)
     demodulation = lax.rsqrt(energy + epsilon)
-    factor = demodulation[:, :, None]
+    factor = demodulation[:, None, :]
 
     smem = pl.BlockSpec(memory_space=pltpu.SMEM)
     work = 2 * TAPS * inputs * outputs * pixels
@@ -346,7 +351,7 @@
         in_specs=[
             smem,
             pl.BlockSpec((1, outputs, pixels), one),
-            pl.BlockSpec((1, outputs, 1), one),
+            pl.BlockSpec((1, 1, outputs), one),
             pl.BlockSpec(by_input.shape, whole),
         ],
         out_specs=[pl.BlockSpec((1, block, pixels), one)] * n,
@@ -376,7 +381,7 @@
         in_specs=[
             smem,
             pl.BlockSpec((1, outputs, pixels), one),
-            pl.BlockSpec((1, outputs, 1), one),
+            pl.BlockSpec((1, 1, outputs), one),
             pl.BlockSpec(squares.shape, whole),
             pl.BlockSpec(by_input.shape, whole),
         ]

time: 120 us -> 120 us (level)
  transfers between devices with their start and end apart: 3 -> 3, of which waited for: 0 -> 1; matrix products, arithmetic and copies ran while one was open for 4% -> 4% of each run, Pallas kernels for 84% -> 83%
where the time goes in v5:
time: 120 us
  Pallas kernels  104 us (87%)
  starting transfers between devices  5.39 us (4%)
  local copies, waits for them, and re-layouts  4.83 us (4%)
  matrix products  3.03 us (3%)
  other arithmetic  1.31 us (1%)
    pallas_call x1, Pallas kernels, on_device(): pl.pallas_call(functools.partial(forward_kernel, side, n), grid=(batch,),...  27.2 us
    pallas_call x1, Pallas kernels, reduce_rows(): pl.pallas_call(functools.partial(reduce_kernel, size, parts, scale), out_...  25.7 us
    pallas_call x1, Pallas kernels, gather_rows(): pl.pallas_call(functools.partial(gather_kernel, size, parts, TAPS), out_s...  25.1 us
    pallas_call x1, Pallas kernels, on_device(): pl.pallas_call(functools.partial(back_kernel, side, n), grid=(batch,), ou...  16.3 us
    ppermute x3, starting transfers between devices, send(): return lax.ppermute(values, 'cout', [(j, (j + step) % n) for j in range(n)])  5.39 us
    pallas_call x1, Pallas kernels, on_device(): pl.pallas_call(finish_kernel, grid=(batch,), out_shape=[jax.ShapeDtypeStr...  5.13 us
    pallas_call x1, Pallas kernels, on_device(): pl.pallas_call(modulate_kernel, grid=(batch,), out_shape=jax.ShapeDtypeSt...  4.11 us
  transfers between devices with their start and end apart: 3, of which 1 were waited for; matrix products, arithmetic and copies ran while one was open for 4% of the time, Pallas kernels for 83%

profile of v5, /device:TPU:0, one launch (start us, length us, event | category | flops | bytes accessed | tf_op | source)
XLA Modules:
  0.0 119.7 jit_solution(15058561662027789102)
XLA Ops:
  0.6 0.7 constant_dynamic-slice_fusion.1
  1.3 0.6 broadcast_in_dim.7.styles_ref
  1.9 4.1 %modulate.1.after_ref.rest_0_ = bf16[4,1024,256]{2,1,0:T(8,128)(2,1)} custom-call(bf16[4,256,1024]{2,1,0:T(8,128)(2,1)} %images_ref.3, f32[4,1,256]{2,1,0:T(1,128)} %broadcast_in_dim.7.styles_ref), custom_call_target="tpu_custom_call" | custom-call | tf_op jit(solution)/shard_map/modulate/pallas_call | solution.py:322
  6.0 2.9 %collective-permute-start = (bf16[4,1024,256]{2,1,0:T(8,128)(2,1)}, bf16[4,1024,256]{2,1,0:T(8,128)(2,1)}, u32[]{:S(2)}, u32[]{:S(2)}) collective-permute-start(bf16[4,1024,256]{2,1,0:T(8,128)(2,1)} %modulate.1.after_ref.rest_0_), channel_id=1, source_target_pairs={{0,1},{1,0},{2,3},{3,2},{4,5},{5,4},{6,7},{7,6},{8,9},{9,8},{10,11... | collective-permute-start | bytes 6291464 | tf_op jit(solution)/shard_map/ppermute | solution.py:316
  9.0 0.0 copy-done.3
  9.0 0.1 copy.8
  9.1 25.1 %gather.1 = (bf16[16,32,2304]{2,1,0:T(8,128)(2,1)}, f32[16,32,256]{2,1,0:T(8,128)}) custom-call(bf16[9,32,256]{2,1,0:T(8,128)(2,1)} %bitcast.16, bf16[4,1024,256]{2,1,0:T(8,128)(2,1)} %modulate.1.after_ref.rest_0_), custom_call_target="tpu_custom_call" | custom-call | tf_op jit(solution)/shard_map/gather/pallas_call | solution.py:278
  34.2 1.6 %fusion.1 = f32[4,256]{1,0:T(4,128)S(1)} fusion(f32[512,256]{1,0:T(8,128)} %bitcast.14, f32[4,512]{0,1:T(8,128)S(1)} %copy.8), kind=kOutput, calls=%fused_computation.3 | convolution fusion | flops 6294528 | bytes 536576 | tf_op jit(solution)/shard_map/dot_general | solution.py:339
  35.8 0.6 broadcast_in_dim.8.factor_ref
  36.4 16.3 %back.1 = (bf16[4,256,1024]{2,1,0:T(8,128)(2,1)}, bf16[4,256,1024]{2,1,0:T(8,128)(2,1)}) custom-call(s32[1]{0:T(128)} %bitcast.me_ref, bf16[4,256,1024]{2,1,0:T(8,128)(2,1)} %upstream_ref.3, f32[4,1,256]{2,1,0:T(1,128)} %broadcast_in_dim.8.factor_ref, bf16[512,2304]{1,0:T(8,128)(2,1)} %bitcast.17), custom_call_target="tpu_custom_call" | custom-call | flops 9663676416 | bytes 8388608 | tf_op jit(solution)/shard_map/back/pallas_call | solution.py:347
  52.7 0.5 collective-permute-start.1
  53.3 0.7 pad.4.squares_ref
  54.0 0.9 collective-permute-done.rest_1_
  54.9 27.2 %forward.1 = (bf16[4,256,1024]{2,1,0:T(8,128)(2,1)}, f32[256,128]{1,0:T(8,128)}, bf16[512,2304]{1,0:T(8,128)(2,1)}) custom-call(s32[1]{0:T(128)} %bitcast.me_ref, bf16[4,256,1024]{2,1,0:T(8,128)(2,1)} %upstream_ref.3, f32[4,1,256]{2,1,0:T(1,128)} %broadcast_in_dim.8.factor_ref, f32[512,128]{1,0:T(8,128)} %pad.4.squares_ref, bf16[512,2304]{1,0:T(8,128)(2,1)} %bitcast.18, ...), custom_call_target="tpu_custom_call" | custom-call | flops 19327352832 | bytes 16777216 | tf_op jit(solution)/shard_map/forward/pallas_call | solution.py:373
  82.2 0.0 copy-done.1
  82.2 1.4 %fusion = bf16[4,512]{1,0:T(4,128)(2,1)S(1)} fusion(f32[512,256]{1,0:T(8,128)S(1)} %bitcast.15, f32[256,128]{1,0:T(8,128)} %get-tuple-element.21, f32[4,512]{1,0:T(4,128)S(1)} %copy-done.3), kind=kOutput, calls=%fused_computation.1 | convolution fusion | flops 6297600 | bytes 667648 | tf_op jit(solution)/shard_map/dot_general | solution.py:412
  83.6 1.9 %collective-permute-start.2 = (bf16[4,256]{1,0:T(4,128)(2,1)S(1)}, bf16[4,256]{1,0:T(4,128)(2,1)S(1)}, u32[]{:S(2)}, u32[]{:S(2)}) collective-permute-start(bf16[4,256]{1,0:T(4,128)(2,1)S(1)} %constant_dynamic-slice_fusion), channel_id=1, source_target_pairs={{0,1},{1,0},{2,3},{3,2},{4,5},{5,4},{6,7},{7,6},{8,9},{9,8},{10,11... | collective-permute-start | bytes 6152 | tf_op jit(solution)/shard_map/ppermute | solution.py:316
  85.6 25.7 %reduce.1.after_ref = f32[9,32,256]{2,1,0:T(8,128)} custom-call(bf16[16,32,2304]{2,1,0:T(8,128)(2,1)} %bitcast.13), custom_call_target="tpu_custom_call" | custom-call | tf_op jit(solution)/shard_map/reduce/pallas_call | solution.py:296
  111.2 0.0 collective-permute-done.1.rest_1_
  111.3 1.3 %copy-done.2 = bf16[4,256,1024]{2,1,0:T(8,128)(2,1)} copy-done((bf16[4,256,1024]{2,1,0:T(8,128)(2,1)}, bf16[4,256,1024]{2,1,0:T(8,128)(2,1)S(1)}, u32[]{:S(2)}) %copy-start.2) | copy-done | bytes 2097176
  112.6 5.1 %finish.1 = (bf16[4,256,1024]{2,1,0:T(8,128)(2,1)}, f32[4,1,256]{2,1,0:T(1,128)}) custom-call(f32[9,32,256]{2,1,0:T(8,128)} %reduce.1.after_ref, bf16[4,256,1024]{2,1,0:T(8,128)(2,1)} %images_ref.3, f32[4,1,256]{2,1,0:T(1,128)} %broadcast_in_dim.7.styles_ref, bf16[4,256,1024]{2,1,0:T(8,128)(2,1)} %get-tuple-element.17.rest_0_, bf16[4,256,1024]{2,1,0:T(8,128)(2,1)} %copy-done.2), custom_call_target="tpu_custom_call" | custom-call | tf_op jit(solution)/shard_map/finish/pallas_call | solution.py:419
  117.7 0.0 collective-permute-done.2
  117.7 1.3 %bitcast_add_fusion = f32[4,256]{1,0:T(4,128)} fusion(f32[4,1,256]{2,1,0:T(1,128)} %get-tuple-element.20, bf16[4,256]{1,0:T(4,128)(2,1)S(1)} %collective-permute-done.2, bf16[4,512]{1,0:T(4,128)(2,1)S(1)} %fusion, s32[]{:T(128)S(6)} %select_n.10), kind=kLoop, calls=%fused_computation.7 | loop fusion | flops 4096 | bytes 12292 | tf_op jit(solution)/shard_map/add | solution.py:432
  119.0 0.7 copy.13
  (7 shorter events, 0.0 us)
Async XLA Ops:
  1.9 7.1 %copy-start.3 = (f32[4,512]{1,0:T(4,128)S(1)}, f32[4,512]{1,0:T(4,128)}, u32[]{:S(2)}) copy-start(f32[4,512]{1,0:T(4,128)} %param.5) | copy-start | bytes 24580
  6.0 48.9 %collective-permute-start = (bf16[4,1024,256]{2,1,0:T(8,128)(2,1)}, bf16[4,1024,256]{2,1,0:T(8,128)(2,1)}, u32[]{:S(2)}, u32[]{:S(2)}) collective-permute-start(bf16[4,1024,256]{2,1,0:T(8,128)(2,1)} %modulate.1.after_ref.rest_0_), channel_id=1, source_target_pairs={{0,1},{1,0},{2,3},{3,2},{4,5},{5,4},{6,7},{7,6},{8,9},{9,8},{10,11... | collective-permute-start | bytes 6291464 | tf_op jit(solution)/shard_map/ppermute | solution.py:316
  52.7 58.6 %collective-permute-start.1 = (bf16[4,256,1024]{2,1,0:T(8,128)(2,1)}, bf16[4,256,1024]{2,1,0:T(8,128)(2,1)S(1)}, u32[]{:S(2)}, u32[]{:S(2)}) collective-permute-start(bf16[4,256,1024]{2,1,0:T(8,128)(2,1)} %get-tuple-element.18), channel_id=1, source_target_pairs={{0,1},{1,0},{2,3},{3,2},{4,5},{5,4},{6,7},{7,6},{8,9},{9,8},{10,11... | collective-permute-start | bytes 6291464 | tf_op jit(solution)/shard_map/ppermute | solution.py:316
  54.0 28.2 %copy-start.1 = (f32[16,32,256]{2,1,0:T(8,128)S(1)}, f32[16,32,256]{2,1,0:T(8,128)}, u32[]{:S(2)}) copy-start(f32[16,32,256]{2,1,0:T(8,128)} %get-tuple-element.13) | copy-start | bytes 1572868
  83.6 34.1 %collective-permute-start.2 = (bf16[4,256]{1,0:T(4,128)(2,1)S(1)}, bf16[4,256]{1,0:T(4,128)(2,1)S(1)}, u32[]{:S(2)}, u32[]{:S(2)}) collective-permute-start(bf16[4,256]{1,0:T(4,128)(2,1)S(1)} %constant_dynamic-slice_fusion), channel_id=1, source_target_pairs={{0,1},{1,0},{2,3},{3,2},{4,5},{5,4},{6,7},{7,6},{8,9},{9,8},{10,11... | collective-permute-start | bytes 6152 | tf_op jit(solution)/shard_map/ppermute | solution.py:316
  111.3 1.3 %copy-start.2 = (bf16[4,256,1024]{2,1,0:T(8,128)(2,1)}, bf16[4,256,1024]{2,1,0:T(8,128)(2,1)S(1)}, u32[]{:S(2)}) copy-start(bf16[4,256,1024]{2,1,0:T(8,128)(2,1)S(1)} %collective-permute-done.1.rest_1_) | copy-start | bytes 6291460
  112.6 6.4 %copy-start = (f32[9,32,256]{2,1,0:T(8,128)S(1)}, f32[9,32,256]{2,1,0:T(8,128)}, u32[]{:S(2)}) copy-start(f32[9,32,256]{2,1,0:T(8,128)} %reduce.1.after_ref) | copy-start | bytes 884740
